TPU v7x, 256 devices: a whole 4x4x8 slice. The times are simulated.
256 devices in a mesh: rows: 64 (over y, z, core), rhs: 4 (over x).
Axes of the slice: x: 4, y: 4, z: 8, core: 2. Of those that a mesh axis runs over, the one named last changes fastest.
Arguments:
- right_side: bfloat16 [512, 512, 256], P('rows', 'rhs'), may hold values from -6 to 6
- off_blocks: bfloat16 [512, 8, 256, 256], P('rows', None, 'rhs'), may hold values from -0.125 to 0.125
- diag_inverse: bfloat16 [512, 256, 256], P('rows', 'rhs'), may hold values from -0.375 to 0.375
- block_level: int32 [512], P('rows'), may hold values from 0 to 3, as said below
- block_columns: int32 [512, 8], P('rows'), may hold values from 0 to 511, as said below
Outputs:
- solved: bfloat16 [512, 512, 256], P('rows', 'rhs')
Inputs may be any that keep to these rules, and one draw needn't show every extreme that they name: `block_level`: among the 8 block rows of one index of rows every level occurs, none more than 4 times, and one level exactly 4 times. `block_columns`: block row i lies on index i // 8 of rows; each of its 8 block columns is a block row on the same index or one of the 3 indices below it (none below 0), of lower level when block row i has level 1 or more. Columns of one block row may repeat.
All inputs are finite; a program needn't handle non-finite values.
Results may differ from a plain program's by a relative error of at most 0.0075.
Values may be sent and summed in bfloat16 or wider, within the bound.
No kernel may reach another device: no remote copies, remote signals or barrier semaphores. Data moves between devices by JAX's collectives and lax.ppermute only.
A program may use at most 128 MiB of HBM per device.

v0:
```python
import functools

import jax
import jax.numpy as jnp
from jax import lax
from jax.experimental import pallas as pl
from jax.experimental.pallas import tpu as pltpu
from jax.sharding import PartitionSpec as P

LEVELS = 4
REACH = 4
CAP = 4
ANY = pl.BlockSpec(memory_space=pl.ANY)
SMEM = pl.BlockSpec(memory_space=pltpu.SMEM)
VMEM = pl.BlockSpec(memory_space=pltpu.VMEM)
PARAMS = pltpu.CompilerParams(vmem_limit_bytes=58 * 2**20)

PLACES = {1: range(0, 4), 2: range(1, 6), 3: range(2, 7), 0: range(4, 8)}
CHUNKS = ((0, 2), (2, 4), (4, 6), (6, 7))
FORWARD = (1, -1, 1, -1)


def order_of(level_ref, order_ref):
    at = jnp.int32(0)
    starts = {}
    for level in (1, 2, 3, 0):
        starts[level] = at
        for row in range(8):
            here = level_ref[row] == level

            @pl.when(here)
            def _(at=at, row=row):
                order_ref[at] = jnp.int32(row)

            at = at + here.astype(jnp.int32)
    return starts


def sort_kernel(level_ref, off_ref, *refs):
    chunks, (order_ref, sems) = refs[: len(CHUNKS)], refs[len(CHUNKS) :]
    order_of(level_ref, order_ref)
    copies = []
    for chunk_ref, (low, high) in zip(chunks, CHUNKS):
        for place in range(low, high):
            copies.append(
                pltpu.make_async_copy(off_ref.at[order_ref[place]], chunk_ref.at[place - low], sems.at[place])
            )
    for copy in copies:
        copy.start()
    for copy in copies:
        copy.wait()


def sort_call(level, off):
    return pl.pallas_call(
        sort_kernel,
        out_shape=[jax.ShapeDtypeStruct((high - low,) + off.shape[1:], off.dtype) for low, high in CHUNKS],
        in_specs=[SMEM, ANY],
        out_specs=[VMEM] * len(CHUNKS),
        scratch_shapes=[pltpu.SMEM((8,), jnp.int32), pltpu.SemaphoreType.DMA((8,))],
        compiler_params=pltpu.CompilerParams(vmem_limit_bytes=60 * 2**20),
    )(level, off)


TABLE = 80
TAIL = 16


def table_kernel(rows_at_ref, x_ref, level_ref, columns_ref, one_ref, two_ref, three_ref, table_ref, slot_ref, levels_ref, near_ref, sem):
    parts = [
        ref[ref.shape[0] - TAIL :, :128].astype(jnp.float32).astype(jnp.int32)[:8] for ref in (one_ref, two_ref, three_ref)
    ]
    lane = lax.broadcasted_iota(jnp.int32, (8, 128), 0)
    levels_ref[...] = jnp.where(lane == 0, parts[0], jnp.where(lane == 1, parts[1], parts[2]))
    copy = pltpu.make_async_copy(levels_ref, near_ref, sem)
    copy.start()
    starts = order_of(level_ref, table_ref)
    ends = {1: starts[2], 2: starts[3], 3: starts[0], 0: jnp.int32(8)}
    for level in range(LEVELS):
        table_ref[8 + level] = starts[level]
        table_ref[12 + level] = ends[level]
    copy.wait()
    for buffer in range(REACH):
        seen = [jnp.int32(0)] * LEVELS
        for row in range(8):
            level = level_ref[row] if buffer == 0 else near_ref[buffer - 1, row] & 3
            rank = jnp.int32(0)
            for other in range(LEVELS):
                here = level == other
                rank = jnp.where(here, seen[other], rank)
                seen[other] = seen[other] + here.astype(jnp.int32)
            slot_ref[buffer * 8 + row] = 16 * jnp.minimum(level, 2) + 4 * buffer + jnp.minimum(rank, CAP - 1)
    base = rows_at_ref[0]
    table_ref[72] = x_ref[0]
    for place in range(7):
        row = table_ref[place]
        for k in range(8):
            column = columns_ref[row, k]
            distance = jnp.clip(base - lax.shift_right_logical(column, 3), 0, REACH - 1)
            buffer = jnp.where((base & distance & 1) == 1, 4 - distance, distance)
            table_ref[16 + 8 * place + k] = slot_ref[buffer * 8 + (column & 7)]


def table_call(rows_at, x_at, level, columns, received):
    return pl.pallas_call(
        table_kernel,
        out_shape=jax.ShapeDtypeStruct((TABLE,), jnp.int32),
        in_specs=[SMEM] * 4 + [VMEM] * 3,
        out_specs=SMEM,
        scratch_shapes=[
            pltpu.SMEM((32,), jnp.int32),
            pltpu.VMEM((8, 128), jnp.int32),
            pltpu.SMEM((8, 128), jnp.int32),
            pltpu.SemaphoreType.DMA,
        ],
        compiler_params=PARAMS,
        cost_estimate=pl.CostEstimate(flops=10**9, bytes_accessed=2**20, transcendentals=0),
    )(rows_at, x_at, level, columns, *received)


def dot_t(x, y):
    return lax.dot_general(x, y, (((1,), (1,)), ((), ())), preferred_element_type=jnp.float32)


def first_kernel(
    x_ref, level_ref, right_ref, own_ref, before_ref, after_ref, low_ref, high_ref,
    out_ref, diag_ref, solved_ref,
    order_ref, inverse, right_buf, solved_buf, tail_buf, sems, right_sems, out_sems, diag_sem, tail_sem,
):
    x_at = x_ref[0]
    columns = right_ref.shape[1]
    half = low_ref.shape[0]
    whole, low, high = pl.ds(0, 2 * half), pl.ds(0, half), pl.ds(half, half)
    sources = ((own_ref, 0, whole), (before_ref, 3, whole), (after_ref, 1, whole), (low_ref, 2, low), (high_ref, 2, high))
    pieces = []
    for n, (ref, turn, rows) in enumerate(sources):
        at = pl.multiple_of(lax.rem(x_at + turn, 4) * 64, 64)
        pieces.append(pltpu.make_async_copy(ref, inverse.at[rows, pl.ds(at, 64)], sems.at[n]))
    for piece in pieces:
        piece.start()
    begin = order_of(level_ref, order_ref)[0]

    def fetch(place):
        return pltpu.make_async_copy(
            right_ref.at[order_ref[place]], right_buf.at[place - 4], right_sems.at[place - 4]
        )

    def stores(place):
        at = pl.multiple_of((place - begin) * columns, columns)
        source = solved_buf.at[place - 4]
        return [
            pltpu.make_async_copy(source, solved_ref.at[pl.ds(at, columns)], out_sems.at[place - 4, 0]),
            pltpu.make_async_copy(source, out_ref.at[order_ref[place]], out_sems.at[place - 4, 1]),
        ]

    for place in PLACES[0]:

        @pl.when(place >= begin)
        def _(place=place):
            fetch(place).start()

    lane = lax.broadcasted_iota(jnp.int32, (TAIL, 256), 1)
    tail = jnp.zeros((TAIL, 256), jnp.int32)
    for row in range(8):
        tail = jnp.where(lane == row, level_ref[row], tail)
    tail_buf[...] = tail.astype(jnp.float32).astype(tail_buf.dtype)
    levels = pltpu.make_async_copy(tail_buf, solved_ref.at[pl.ds(CAP * columns, TAIL)], tail_sem)
    levels.start()
    for piece in pieces:
        piece.wait()
    whole = pltpu.make_async_copy(inverse, diag_ref, diag_sem)
    whole.start()
    for place in PLACES[0]:

        @pl.when(place >= begin)
        def _(place=place):
            fetch(place).wait()
            solved_buf[place - 4] = dot_t(right_buf[place - 4], inverse[order_ref[place]]).astype(solved_buf.dtype)
            for copy in stores(place):
                copy.start()

    for place in PLACES[0]:

        @pl.when(place >= begin)
        def _(place=place):
            for copy in stores(place):
                copy.wait()

    levels.wait()
    whole.wait()


def first_call(x_at, level, right, diag_pieces):
    rows, columns, size = right.shape
    return pl.pallas_call(
        first_kernel,
        out_shape=[
            jax.ShapeDtypeStruct(right.shape, right.dtype),
            jax.ShapeDtypeStruct((rows, size, size), right.dtype),
            jax.ShapeDtypeStruct((CAP * columns + TAIL, size), right.dtype),
        ],
        in_specs=[SMEM, SMEM] + [ANY] * 6,
        out_specs=[ANY, ANY, ANY],
        scratch_shapes=[
            pltpu.SMEM((8,), jnp.int32),
            pltpu.VMEM((rows, size, size), right.dtype),
            pltpu.VMEM((CAP, columns, size), right.dtype),
            pltpu.VMEM((CAP, columns, size), right.dtype),
            pltpu.VMEM((TAIL, size), right.dtype),
            pltpu.SemaphoreType.DMA((5,)),
            pltpu.SemaphoreType.DMA((CAP,)),
            pltpu.SemaphoreType.DMA((CAP, 2)),
            pltpu.SemaphoreType.DMA,
            pltpu.SemaphoreType.DMA,
        ],
        compiler_params=PARAMS,
        cost_estimate=pl.CostEstimate(flops=2 * CAP * columns * size * size, bytes_accessed=3 * 2**20, transcendentals=0),
    )(x_at, level, right, *diag_pieces)


def chunk_of(place):
    return next(n for n, (low, high) in enumerate(CHUNKS) if low <= place < high)


def level_kernel(level, used, table_ref, right_ref, diag_ref, *refs):
    places = PLACES[level]
    refs = list(refs)

    def take(count):
        taken = refs[:count]
        del refs[:count]
        return taken

    parts = {n: take(4) for n in used}
    windows = take(4 * level)
    take(1)
    out_ref = take(1)[0]
    solved_ref = take(1)[0] if level < LEVELS - 1 else None
    window, factor, diag_buf, right_buf, solved_buf, totals, window_sems, factor_sems, row_sems, out_sems = refs
    columns = right_ref.shape[1]
    x_at = table_ref[72]
    begin, end = table_ref[8 + level], table_ref[12 + level]

    def fetches(place):
        slot = place - places[0]
        row = table_ref[place]
        copies = [
            pltpu.make_async_copy(right_ref.at[row], right_buf.at[slot], row_sems.at[slot, 0]),
            pltpu.make_async_copy(diag_ref.at[row], diag_buf.at[slot], row_sems.at[slot, 1]),
        ]
        n = chunk_of(place)
        for quarter, (ref, turn) in enumerate(zip(parts[n], (0, 3, 1, 2))):
            source = ref.at[place - CHUNKS[n][0]]
            target = factor.at[slot, :, pl.ds(pl.multiple_of(lax.rem(x_at + turn, 4) * 64, 64), 64), :]
            copies.append(pltpu.make_async_copy(source, target, factor_sems.at[slot, quarter]))
        return copies

    def stores(place):
        slot = place - places[0]
        copies = [pltpu.make_async_copy(solved_buf.at[slot], out_ref.at[table_ref[place]], out_sems.at[slot, 0])]
        if solved_ref is not None:
            at = pl.multiple_of((place - begin) * columns, columns)
            copies.append(
                pltpu.make_async_copy(solved_buf.at[slot], solved_ref.at[pl.ds(at, columns)], out_sems.at[slot, 1])
            )
        return copies

    incoming = [
        pltpu.make_async_copy(
            ref.at[pl.ds(0, CAP * columns)], window.at[pl.ds(n * CAP * columns, CAP * columns)], window_sems.at[n]
        )
        for n, ref in enumerate(windows)
    ]
    for copy in incoming:
        copy.start()
    for place in places:

        @pl.when((place >= begin) & (place < end))
        def _(place=place):
            for copy in fetches(place):
                copy.start()

    for copy in incoming:
        copy.wait()
    for place in places:

        @pl.when((place >= begin) & (place < end))
        def _(place=place):
            slot = place - places[0]
            for copy in fetches(place):
                copy.wait()
            total = jnp.zeros(right_buf.shape[1:], jnp.float32)
            for k in range(8):
                at = pl.multiple_of(table_ref[16 + 8 * place + k] * columns, columns)
                total = total + dot_t(window[pl.ds(at, columns)], factor[slot, k])
            totals[slot] = total

    for place in places:
        slot = place - places[0]
        residue = (right_buf[slot].astype(jnp.float32) - totals[slot]).astype(jnp.bfloat16)
        solved_buf[slot] = dot_t(residue, diag_buf[slot]).astype(solved_buf.dtype)
    for place in places:

        @pl.when((place >= begin) & (place < end))
        def _(place=place):
            for copy in stores(place):
                copy.start()

    for place in places:

        @pl.when((place >= begin) & (place < end))
        def _(place=place):
            for copy in stores(place):
                copy.wait()


def level_call(level, table, right, diag, parts, windows, out):
    rows, columns, size = right.shape
    places = PLACES[level]
    used = sorted({chunk_of(place) for place in places})
    flat = [piece for n in used for piece in parts[n]]
    operands = [table, right, diag, *flat, *windows, out]
    count = len(places)
    return pl.pallas_call(
        functools.partial(level_kernel, level, used),
        out_shape=[
            jax.ShapeDtypeStruct(out.shape, out.dtype),
            jax.ShapeDtypeStruct((CAP * columns, size), out.dtype),
        ][: 1 if level == LEVELS - 1 else 2],
        in_specs=[SMEM] + [ANY] * (len(operands) - 1),
        out_specs=[ANY, ANY][: 1 if level == LEVELS - 1 else 2],
        input_output_aliases={len(operands) - 1: 0},
        scratch_shapes=[
            pltpu.VMEM((4 * level * CAP * columns, size), out.dtype),
            pltpu.VMEM((count, 8, size, size), out.dtype),
            pltpu.VMEM((count, size, size), out.dtype),
            pltpu.VMEM((count, columns, size), out.dtype),
            pltpu.VMEM((count, columns, size), out.dtype),
            pltpu.VMEM((count, columns, size), jnp.float32),
            pltpu.SemaphoreType.DMA((4 * level,)),
            pltpu.SemaphoreType.DMA((count, 4)),
            pltpu.SemaphoreType.DMA((count, 2)),
            pltpu.SemaphoreType.DMA((count, 2)),
        ],
        compiler_params=PARAMS,
        cost_estimate=pl.CostEstimate(
            flops=2 * CAP * 9 * columns * size * size, bytes_accessed=8 * 2**20, transcendentals=0
        ),
    )(*operands)


def round_x(block, distance):
    size = lax.axis_size("rhs")
    return lax.ppermute(block, "rhs", [(i, (i + distance) % size) for i in range(size)])


def up(block, distance):
    size = lax.axis_size("rows")
    return lax.ppermute(block, "rows", [(i, i + distance) for i in range(size - distance)])


def after(value, *others):
    return lax.optimization_barrier((value, others))[0]


def ring(chunk, forward, *before):
    low, high = round_x(chunk, 1), round_x(chunk, -1)
    if forward == 0:
        return [chunk, low, high, round_x(chunk, 2)]
    return [chunk, low, high, round_x(after(low if forward > 0 else high, *before), forward)]


def shift(solved):
    size = lax.axis_size("rows")
    two = up(solved, 2)
    mixed = lax.ppermute(
        solved, "rows", [(i, i + (3 if i % 2 else 1)) for i in range(size) if i + (3 if i % 2 else 1) < size]
    )
    swapped = lax.ppermute(after(two, mixed), "rows", [(i, i ^ 1) for i in range(size)])
    return [solved, swapped, two, mixed]


def per_device(right, off, diag, level, columns):
    x_at = lax.axis_index("rhs").astype(jnp.int32).reshape(1)
    rows_at = lax.axis_index("rows").astype(jnp.int32).reshape(1)
    half = diag.shape[0] // 2
    before, beyond = round_x(diag, 1), round_x(diag, -1)
    chunks = sort_call(level, off)
    low, high = after((before[:half], beyond[half:]), *chunks)
    diag_pieces = [diag, before, beyond, round_x(low, 1), round_x(high, -1)]
    out, diag, solved = first_call(x_at, level, right, diag_pieces)
    windows = shift(solved)
    parts = []
    for chunk, ahead in ((chunks[0], []), (chunks[1], [*diag_pieces])):
        chunk = after(chunk, *ahead)
        parts.append([chunk, round_x(chunk, 1), round_x(chunk, -1)])
    ahead = [solved, *parts[0], *parts[1]]
    parts[0].append(round_x(after(parts[0][1], solved), 1))
    parts[1].append(round_x(after(parts[1][2], *ahead), -1))
    table = table_call(rows_at, x_at, level, columns, windows[1:])
    parts.append(ring(after(chunks[2], *parts[1], *parts[0], table), FORWARD[2]))
    out, solved = level_call(1, table, right, diag, parts, windows, out)
    windows += shift(solved)
    parts.append(ring(after(chunks[3], *parts[2][:3]), FORWARD[3]))
    out, solved = level_call(2, table, right, diag, parts, windows, out)
    windows += shift(solved)
    return level_call(3, table, right, diag, parts, windows, out)[0]


def solution(mesh):
    return jax.shard_map(
        per_device,
        mesh=mesh,
        in_specs=(
            P("rows", "rhs", None),
            P("rows", None, "rhs", None),
            P("rows", "rhs", None),
            P("rows"),
            P("rows", None),
        ),
        out_specs=P("rows", "rhs", None),
        check_vma=False,
    )
```

profile of v0, /device:TPU:8, one launch (start us, length us, event | category | flops | bytes accessed | tf_op | source)
XLA Modules:
  0.0 115.4 jit_solution(5195030565786330046)
XLA Ops:
  0.0 1.5 %collective-permute-start = (bf16[8,64,256]{2,1,0:T(8,128)(2,1)}, bf16[8,64,256]{2,1,0:T(8,128)(2,1)S(1)}, u32[]{:S(2)}, u32[]{:S(2)}) collective-permute-start(bf16[8,64,256]{2,1,0:T(8,128)(2,1)} %own_ref.1), channel_id=1, source_target_pairs={{0,1},{1,2},{2,3},{3,0},{4,5},{5,6},{6,7},{7,4},{8,9},{9,10},{10,1... | collective-permute-start | bytes 786440 | tf_op jit(solution)/shard_map/ppermute | solution.py:354
  1.5 1.7 %collective-permute-start.1 = (bf16[8,64,256]{2,1,0:T(8,128)(2,1)}, bf16[8,64,256]{2,1,0:T(8,128)(2,1)S(1)}, u32[]{:S(2)}, u32[]{:S(2)}) collective-permute-start(bf16[8,64,256]{2,1,0:T(8,128)(2,1)} %own_ref.1), channel_id=1, source_target_pairs={{0,3},{1,0},{2,1},{3,2},{4,7},{5,4},{6,5},{7,6},{8,11},{9,8},{10,9... | collective-permute-start | bytes 786440 | tf_op jit(solution)/shard_map/ppermute | solution.py:354
  3.2 3.4 %shard_map.55 = (bf16[2,8,64,256]{3,2,1,0:T(8,128)(2,1)}, bf16[2,8,64,256]{3,2,1,0:T(8,128)(2,1)}, bf16[2,8,64,256]{3,2,1,0:T(8,128)(2,1)}, bf16[1,8,64,256]{3,2,1,0:T(8,128)(2,1)}) custom-call(s32[8]{0:T(128)} %level_ref.5, bf16[8,8,64,256]{3,2,1,0:T(8,128)(2,1)} %off_ref.1), custom_call_target="tpu_custom_call" | custom-call | tf_op jit(solution)/shard_map/pallas_call | solution.py:55
  6.7 2.8 %collective-permute-done.before_ref = bf16[8,64,256]{2,1,0:T(8,128)(2,1)S(1)} collective-permute-done((bf16[8,64,256]{2,1,0:T(8,128)(2,1)}, bf16[8,64,256]{2,1,0:T(8,128)(2,1)S(1)}, u32[]{:S(2)}, u32[]{:S(2)}) %collective-permute-start) | collective-permute-done | bytes 262176 | tf_op jit(solution)/shard_map/ppermute | solution.py:354
  9.5 0.0 collective-permute-done.1.after_ref
  9.5 1.5 %collective-permute-start.2 = (bf16[4,64,256]{2,1,0:T(8,128)(2,1)S(1)}, bf16[4,64,256]{2,1,0:T(8,128)(2,1)S(1)}, u32[]{:S(2)}, u32[]{:S(2)}) collective-permute-start(bf16[4,64,256]{2,1,0:T(8,128)(2,1)S(1)} %slice.8), channel_id=1, source_target_pairs={{0,1},{1,2},{2,3},{3,0},{4,5},{5,6},{6,7},{7,4},{8,9},{9,10},{10,1... | collective-permute-start | bytes 393224 | tf_op jit(solution)/shard_map/ppermute | solution.py:354
  11.1 1.8 %collective-permute-start.3 = (bf16[4,64,256]{2,1,0:T(8,128)(2,1)S(1)}, bf16[4,64,256]{2,1,0:T(8,128)(2,1)S(1)}, u32[]{:S(2)}, u32[]{:S(2)}) collective-permute-start(bf16[4,64,256]{2,1,0:T(8,128)(2,1)S(1)} %slice.9), channel_id=1, source_target_pairs={{0,3},{1,0},{2,1},{3,2},{4,7},{5,4},{6,5},{7,6},{8,11},{9,8},{10,9... | collective-permute-start | bytes 393224 | tf_op jit(solution)/shard_map/ppermute | solution.py:354
  12.8 0.2 collective-permute-start.9
  13.1 3.0 %collective-permute-start.10 = (bf16[2,8,64,256]{3,2,1,0:T(8,128)(2,1)}, bf16[2,8,64,256]{3,2,1,0:T(8,128)(2,1)S(1)}, u32[]{:S(2)}, u32[]{:S(2)}) collective-permute-start(bf16[2,8,64,256]{3,2,1,0:T(8,128)(2,1)} %get-tuple-element.26.refs_0_), channel_id=1, source_target_pairs={{0,3},{1,0},{2,1},{3,2},{4,7},{5,4},{6,5},{7,6},{8,11},{9,8},{10,9... | collective-permute-start | bytes 1572872 | tf_op jit(solution)/shard_map/ppermute | solution.py:354
  16.1 0.2 collective-permute-done.2.low_ref
  16.3 1.0 collective-permute-done.3.high_ref
  17.4 1.2 %collective-permute-start.7 = (bf16[2,8,64,256]{3,2,1,0:T(8,128)(2,1)}, bf16[2,8,64,256]{3,2,1,0:T(8,128)(2,1)S(1)}, u32[]{:S(2)}, u32[]{:S(2)}) collective-permute-start(bf16[2,8,64,256]{3,2,1,0:T(8,128)(2,1)} %get-tuple-element.35.refs_4_.refs_0_), channel_id=1, source_target_pairs={{0,1},{1,2},{2,3},{3,0},{4,5},{5,6},{6,7},{7,4},{8,9},{9,10},{10,1... | collective-permute-start | bytes 1572872 | tf_op jit(solution)/shard_map/ppermute | solution.py:354
  18.6 2.0 %collective-permute-start.8 = (bf16[2,8,64,256]{3,2,1,0:T(8,128)(2,1)}, bf16[2,8,64,256]{3,2,1,0:T(8,128)(2,1)S(1)}, u32[]{:S(2)}, u32[]{:S(2)}) collective-permute-start(bf16[2,8,64,256]{3,2,1,0:T(8,128)(2,1)} %get-tuple-element.35.refs_4_.refs_0_), channel_id=1, source_target_pairs={{0,3},{1,0},{2,1},{3,2},{4,7},{5,4},{6,5},{7,6},{8,11},{9,8},{10,9... | collective-permute-start | bytes 1572872 | tf_op jit(solution)/shard_map/ppermute | solution.py:354
  20.6 3.1 %shard_map.56 = (bf16[8,128,256]{2,1,0:T(8,128)(2,1)}, bf16[8,256,256]{2,1,0:T(8,128)(2,1)}, bf16[528,256]{1,0:T(8,128)(2,1)}) custom-call(s32[1]{0:T(128)} %bitcast.1.x_ref, s32[8]{0:T(128)} %level_ref.5, bf16[8,128,256]{2,1,0:T(8,128)(2,1)} %right_ref.7, bf16[8,64,256]{2,1,0:T(8,128)(2,1)} %own_ref.1, bf16[8,64,256]{2,1,0:T(8,128)(2,1)} %copy-done.15, ...), custom_call_target="tpu_custom_call" | custom-call | flops 67108864 | bytes 3145728 | tf_op jit(solution)/shard_map/pallas_call | solution.py:195
  23.7 4.0 %collective-permute-start.4 = (bf16[528,256]{1,0:T(8,128)(2,1)}, bf16[528,256]{1,0:T(8,128)(2,1)S(1)}, u32[]{:S(2)}, u32[]{:S(2)}) collective-permute-start(bf16[528,256]{1,0:T(8,128)(2,1)} %get-tuple-element.32.refs_8_.refs_12_), channel_id=1, source_target_pairs={{0,8},{4,12},{8,16},{12,20},{16,24},{20,28},{24,32},{28,36},{32,40... | collective-permute-start | bytes 811016 | tf_op jit(solution)/shard_map/ppermute | solution.py:359
  27.7 1.4 %collective-permute-done.9.refs_1_ = bf16[2,8,64,256]{3,2,1,0:T(8,128)(2,1)S(1)} collective-permute-done((bf16[2,8,64,256]{3,2,1,0:T(8,128)(2,1)}, bf16[2,8,64,256]{3,2,1,0:T(8,128)(2,1)S(1)}, u32[]{:S(2)}, u32[]{:S(2)}) %collective-permute-start.9) | collective-permute-done | bytes 524320 | tf_op jit(solution)/shard_map/ppermute | solution.py:354
  29.1 1.9 %collective-permute-start.5 = (bf16[528,256]{1,0:T(8,128)(2,1)}, bf16[528,256]{1,0:T(8,128)(2,1)S(1)}, u32[]{:S(2)}, u32[]{:S(2)}) collective-permute-start(bf16[528,256]{1,0:T(8,128)(2,1)} %get-tuple-element.32.refs_8_.refs_12_), channel_id=1, source_target_pairs={{0,4},{4,16},{8,12},{12,24},{16,20},{20,32},{24,28},{28,40},{32,36... | collective-permute-start | bytes 811016 | tf_op jit(solution)/shard_map/ppermute | solution.py:376
  31.1 0.1 collective-permute-start.12
  31.2 7.1 %collective-permute-done.7.refs_5_.refs_1_ = bf16[2,8,64,256]{3,2,1,0:T(8,128)(2,1)S(1)} collective-permute-done((bf16[2,8,64,256]{3,2,1,0:T(8,128)(2,1)}, bf16[2,8,64,256]{3,2,1,0:T(8,128)(2,1)S(1)}, u32[]{:S(2)}, u32[]{:S(2)}) %collective-permute-start.7) | collective-permute-done | bytes 524320 | tf_op jit(solution)/shard_map/ppermute | solution.py:354
  38.3 3.2 %collective-permute-start.11 = (bf16[2,8,64,256]{3,2,1,0:T(8,128)(2,1)S(1)}, bf16[2,8,64,256]{3,2,1,0:T(8,128)(2,1)S(1)}, u32[]{:S(2)}, u32[]{:S(2)}) collective-permute-start(bf16[2,8,64,256]{3,2,1,0:T(8,128)(2,1)S(1)} %collective-permute-done.8.refs_6_.refs_2_), channel_id=1, source_target_pairs={{0,3},{1,0},{2,1},{3,2},{4,7},{5,4},{6,5},{7,6},{8,11},{9,8},{10,9... | collective-permute-start | bytes 1572872 | tf_op jit(solution)/shard_map/ppermute | solution.py:354
  41.5 0.0 collective-permute-done.4.two_ref.refs_10_.refs_14_
  41.5 0.1 collective-permute-start.6
  41.6 1.5 %collective-permute-done.6.one_ref.refs_9_.refs_13_ = bf16[528,256]{1,0:T(8,128)(2,1)S(1)} collective-permute-done((bf16[528,256]{1,0:T(8,128)(2,1)S(1)}, bf16[528,256]{1,0:T(8,128)(2,1)S(1)}, u32[]{:S(2)}, u32[]{:S(2)}) %collective-permute-start.6) | collective-permute-done | bytes 270368 | tf_op jit(solution)/shard_map/ppermute | solution.py:379
  43.2 0.7 copy-done.5
  43.9 2.8 %shard_map.57.table_ref = s32[80]{0:T(128)} custom-call(s32[1]{0:T(128)} %bitcast.rows_at_ref, s32[1]{0:T(128)} %bitcast.1.x_ref, s32[8]{0:T(128)} %level_ref.5, s32[8,8]{1,0:T(8,128)} %columns_ref.1, bf16[528,256]{1,0:T(8,128)(2,1)} %copy-done.5, bf16[528,256]{1,0:T(8,128)(2,1)} %copy-done.3, bf16[528,256]{1,0:T(8,128)(2,1)} %copy-done.4), custom_call_target="tpu_custom_call" | custom-call | flops 1000000000 | bytes 1048576 | tf_op jit(solution)/shard_map/pallas_call | solution.py:105
  46.7 2.8 %collective-permute-done.12.refs_3_ = bf16[2,8,64,256]{3,2,1,0:T(8,128)(2,1)} collective-permute-done((bf16[2,8,64,256]{3,2,1,0:T(8,128)(2,1)S(1)}, bf16[2,8,64,256]{3,2,1,0:T(8,128)(2,1)}, u32[]{:S(2)}, u32[]{:S(2)}) %collective-permute-start.12) | collective-permute-done | bytes 524320 | tf_op jit(solution)/shard_map/ppermute | solution.py:354
  49.5 1.4 %collective-permute-done.11.refs_7_.refs_3_ = bf16[2,8,64,256]{3,2,1,0:T(8,128)(2,1)S(1)} collective-permute-done((bf16[2,8,64,256]{3,2,1,0:T(8,128)(2,1)S(1)}, bf16[2,8,64,256]{3,2,1,0:T(8,128)(2,1)S(1)}, u32[]{:S(2)}, u32[]{:S(2)}) %collective-permute-start.11) | collective-permute-done | bytes 524320 | tf_op jit(solution)/shard_map/ppermute | solution.py:354
  50.8 0.0 collective-permute-start.13
  50.8 3.8 %collective-permute-start.14 = (bf16[2,8,64,256]{3,2,1,0:T(8,128)(2,1)S(1)}, bf16[2,8,64,256]{3,2,1,0:T(8,128)(2,1)S(1)}, u32[]{:S(2)}, u32[]{:S(2)}) collective-permute-start(bf16[2,8,64,256]{3,2,1,0:T(8,128)(2,1)S(1)} %copy-done.6), channel_id=1, source_target_pairs={{0,3},{1,0},{2,1},{3,2},{4,7},{5,4},{6,5},{7,6},{8,11},{9,8},{10,9... | collective-permute-start | bytes 1572872 | tf_op jit(solution)/shard_map/ppermute | solution.py:354
  54.6 4.3 %shard_map.58 = (bf16[8,128,256]{2,1,0:T(8,128)(2,1)}, bf16[512,256]{1,0:T(8,128)(2,1)}) custom-call(s32[80]{0:T(128)} %shard_map.57.table_ref, bf16[8,128,256]{2,1,0:T(8,128)(2,1)} %right_ref.7, bf16[8,256,256]{2,1,0:T(8,128)(2,1)} %get-tuple-element.34.diag_ref, ...), custom_call_target="tpu_custom_call", output_to_operand_aliasing={{0}: (15, {})} | custom-call | flops 603979776 | bytes 8388608 | tf_op jit(solution)/shard_map/pallas_call | solution.py:324
  59.0 3.8 %collective-permute-start.19 = (bf16[512,256]{1,0:T(8,128)(2,1)}, bf16[512,256]{1,0:T(8,128)(2,1)S(1)}, u32[]{:S(2)}, u32[]{:S(2)}) collective-permute-start(bf16[512,256]{1,0:T(8,128)(2,1)} %get-tuple-element.41.refs_16_), channel_id=1, source_target_pairs={{0,8},{4,12},{8,16},{12,20},{16,24},{20,28},{24,32},{28,36},{32,40... | collective-permute-start | bytes 786440 | tf_op jit(solution)/shard_map/ppermute | solution.py:359
  62.8 1.9 %collective-permute-start.20 = (bf16[512,256]{1,0:T(8,128)(2,1)}, bf16[512,256]{1,0:T(8,128)(2,1)S(1)}, u32[]{:S(2)}, u32[]{:S(2)}) collective-permute-start(bf16[512,256]{1,0:T(8,128)(2,1)} %get-tuple-element.41.refs_16_), channel_id=1, source_target_pairs={{0,4},{4,16},{8,12},{12,24},{16,20},{20,32},{24,28},{28,40},{32,36... | collective-permute-start | bytes 786440 | tf_op jit(solution)/shard_map/ppermute | solution.py:376
  64.8 0.1 collective-permute-start.15
  64.9 14.4 %collective-permute-done.19.refs_18_ = bf16[512,256]{1,0:T(8,128)(2,1)S(1)} collective-permute-done((bf16[512,256]{1,0:T(8,128)(2,1)}, bf16[512,256]{1,0:T(8,128)(2,1)S(1)}, u32[]{:S(2)}, u32[]{:S(2)}) %collective-permute-start.19) | collective-permute-done | bytes 262176 | tf_op jit(solution)/shard_map/ppermute | solution.py:359
  79.3 0.1 collective-permute-start.21
  79.4 2.0 %collective-permute-start.17 = (bf16[1,8,64,256]{3,2,1,0:T(8,128)(2,1)S(1)}, bf16[1,8,64,256]{3,2,1,0:T(8,128)(2,1)S(1)}, u32[]{:S(2)}, u32[]{:S(2)}) collective-permute-start(bf16[1,8,64,256]{3,2,1,0:T(8,128)(2,1)S(1)} %copy-done.17), channel_id=1, source_target_pairs={{0,3},{1,0},{2,1},{3,2},{4,7},{5,4},{6,5},{7,6},{8,11},{9,8},{10,9... | collective-permute-start | bytes 786440 | tf_op jit(solution)/shard_map/ppermute | solution.py:354
  81.5 0.7 copy-done.14
  82.2 0.2 copy-done.9
  82.4 5.4 %shard_map.59 = (bf16[8,128,256]{2,1,0:T(8,128)(2,1)}, bf16[512,256]{1,0:T(8,128)(2,1)}) custom-call(s32[80]{0:T(128)} %shard_map.57.table_ref, bf16[8,128,256]{2,1,0:T(8,128)(2,1)} %right_ref.7, bf16[8,256,256]{2,1,0:T(8,128)(2,1)} %get-tuple-element.34.diag_ref, ...), custom_call_target="tpu_custom_call", output_to_operand_aliasing={{0}: (23, {})} | custom-call | flops 603979776 | bytes 8388608 | tf_op jit(solution)/shard_map/pallas_call | solution.py:324
  87.8 2.4 %collective-permute-start.22 = (bf16[512,256]{1,0:T(8,128)(2,1)}, bf16[512,256]{1,0:T(8,128)(2,1)S(1)}, u32[]{:S(2)}, u32[]{:S(2)}) collective-permute-start(bf16[512,256]{1,0:T(8,128)(2,1)} %get-tuple-element.44.refs_20_), channel_id=1, source_target_pairs={{0,8},{4,12},{8,16},{12,20},{16,24},{20,28},{24,32},{28,36},{32,40... | collective-permute-start | bytes 786440 | tf_op jit(solution)/shard_map/ppermute | solution.py:359
  90.2 1.9 %collective-permute-start.23 = (bf16[512,256]{1,0:T(8,128)(2,1)}, bf16[512,256]{1,0:T(8,128)(2,1)S(1)}, u32[]{:S(2)}, u32[]{:S(2)}) collective-permute-start(bf16[512,256]{1,0:T(8,128)(2,1)} %get-tuple-element.44.refs_20_), channel_id=1, source_target_pairs={{0,4},{4,16},{8,12},{12,24},{16,20},{20,32},{24,28},{28,40},{32,36... | collective-permute-start | bytes 786440 | tf_op jit(solution)/shard_map/ppermute | solution.py:376
  92.1 0.2 collective-permute-start.16
  92.3 3.2 %collective-permute-start.18 = (bf16[1,8,64,256]{3,2,1,0:T(8,128)(2,1)S(1)}, bf16[1,8,64,256]{3,2,1,0:T(8,128)(2,1)S(1)}, u32[]{:S(2)}, u32[]{:S(2)}) collective-permute-start(bf16[1,8,64,256]{3,2,1,0:T(8,128)(2,1)S(1)} %collective-permute-done.17.refs_10_), channel_id=1, source_target_pairs={{0,3},{1,0},{2,1},{3,2},{4,7},{5,4},{6,5},{7,6},{8,11},{9,8},{10,9... | collective-permute-start | bytes 786440 | tf_op jit(solution)/shard_map/ppermute | solution.py:354
  95.4 4.9 %collective-permute-done.22.refs_22_ = bf16[512,256]{1,0:T(8,128)(2,1)S(1)} collective-permute-done((bf16[512,256]{1,0:T(8,128)(2,1)}, bf16[512,256]{1,0:T(8,128)(2,1)S(1)}, u32[]{:S(2)}, u32[]{:S(2)}) %collective-permute-start.22) | collective-permute-done | bytes 262176 | tf_op jit(solution)/shard_map/ppermute | solution.py:359
  100.3 5.3 %collective-permute-done.23.refs_23_ = bf16[512,256]{1,0:T(8,128)(2,1)S(1)} collective-permute-done((bf16[512,256]{1,0:T(8,128)(2,1)}, bf16[512,256]{1,0:T(8,128)(2,1)S(1)}, u32[]{:S(2)}, u32[]{:S(2)}) %collective-permute-start.23) | collective-permute-done | bytes 262176 | tf_op jit(solution)/shard_map/ppermute | solution.py:376
  105.6 1.5 %collective-permute-done.24.refs_21_ = bf16[512,256]{1,0:T(8,128)(2,1)S(1)} collective-permute-done((bf16[512,256]{1,0:T(8,128)(2,1)S(1)}, bf16[512,256]{1,0:T(8,128)(2,1)S(1)}, u32[]{:S(2)}, u32[]{:S(2)}) %collective-permute-start.24) | collective-permute-done | bytes 262176 | tf_op jit(solution)/shard_map/ppermute | solution.py:379
  107.2 0.7 copy-done.23
  107.8 7.4 %shard_map.60 = bf16[8,128,256]{2,1,0:T(8,128)(2,1)} custom-call(s32[80]{0:T(128)} %shard_map.57.table_ref, bf16[8,128,256]{2,1,0:T(8,128)(2,1)} %right_ref.7, bf16[8,256,256]{2,1,0:T(8,128)(2,1)} %get-tuple-element.34.diag_ref, bf16[2,8,64,256]{3,2,1,0:T(8,128)(2,1)} %get-tuple-element.35.refs_4_.refs_0_, ...), custom_call_target="tpu_custom_call", output_to_operand_aliasing={{}: (27, {})} | custom-call | flops 603979776 | bytes 8388608 | tf_op jit(solution)/shard_map/pallas_call | solution.py:324
  (62 shorter events, 0.1 us)
Async XLA Ops:
  0.0 9.5 %collective-permute-start = (bf16[8,64,256]{2,1,0:T(8,128)(2,1)}, bf16[8,64,256]{2,1,0:T(8,128)(2,1)S(1)}, u32[]{:S(2)}, u32[]{:S(2)}) collective-permute-start(bf16[8,64,256]{2,1,0:T(8,128)(2,1)} %own_ref.1), channel_id=1, source_target_pairs={{0,1},{1,2},{2,3},{3,0},{4,5},{5,6},{6,7},{7,4},{8,9},{9,10},{10,1... | collective-permute-start | bytes 786440 | tf_op jit(solution)/shard_map/ppermute | solution.py:354
  1.5 8.0 %collective-permute-start.1 = (bf16[8,64,256]{2,1,0:T(8,128)(2,1)}, bf16[8,64,256]{2,1,0:T(8,128)(2,1)S(1)}, u32[]{:S(2)}, u32[]{:S(2)}) collective-permute-start(bf16[8,64,256]{2,1,0:T(8,128)(2,1)} %own_ref.1), channel_id=1, source_target_pairs={{0,3},{1,0},{2,1},{3,2},{4,7},{5,4},{6,5},{7,6},{8,11},{9,8},{10,9... | collective-permute-start | bytes 786440 | tf_op jit(solution)/shard_map/ppermute | solution.py:354
  9.5 11.1 %copy-start.15 = (bf16[8,64,256]{2,1,0:T(8,128)(2,1)}, bf16[8,64,256]{2,1,0:T(8,128)(2,1)S(1)}, u32[]{:S(2)}) copy-start(bf16[8,64,256]{2,1,0:T(8,128)(2,1)S(1)} %collective-permute-done.before_ref) | copy-start | bytes 786436
  9.5 11.1 %copy-start.16 = (bf16[8,64,256]{2,1,0:T(8,128)(2,1)}, bf16[8,64,256]{2,1,0:T(8,128)(2,1)S(1)}, u32[]{:S(2)}) copy-start(bf16[8,64,256]{2,1,0:T(8,128)(2,1)S(1)} %collective-permute-done.1.after_ref) | copy-start | bytes 786436
  9.5 6.8 %collective-permute-start.2 = (bf16[4,64,256]{2,1,0:T(8,128)(2,1)S(1)}, bf16[4,64,256]{2,1,0:T(8,128)(2,1)S(1)}, u32[]{:S(2)}, u32[]{:S(2)}) collective-permute-start(bf16[4,64,256]{2,1,0:T(8,128)(2,1)S(1)} %slice.8), channel_id=1, source_target_pairs={{0,1},{1,2},{2,3},{3,0},{4,5},{5,6},{6,7},{7,4},{8,9},{9,10},{10,1... | collective-permute-start | bytes 393224 | tf_op jit(solution)/shard_map/ppermute | solution.py:354
  11.1 6.3 %collective-permute-start.3 = (bf16[4,64,256]{2,1,0:T(8,128)(2,1)S(1)}, bf16[4,64,256]{2,1,0:T(8,128)(2,1)S(1)}, u32[]{:S(2)}, u32[]{:S(2)}) collective-permute-start(bf16[4,64,256]{2,1,0:T(8,128)(2,1)S(1)} %slice.9), channel_id=1, source_target_pairs={{0,3},{1,0},{2,1},{3,2},{4,7},{5,4},{6,5},{7,6},{8,11},{9,8},{10,9... | collective-permute-start | bytes 393224 | tf_op jit(solution)/shard_map/ppermute | solution.py:354
  12.8 16.3 %collective-permute-start.9 = (bf16[2,8,64,256]{3,2,1,0:T(8,128)(2,1)}, bf16[2,8,64,256]{3,2,1,0:T(8,128)(2,1)S(1)}, u32[]{:S(2)}, u32[]{:S(2)}) collective-permute-start(bf16[2,8,64,256]{3,2,1,0:T(8,128)(2,1)} %get-tuple-element.26.refs_0_), channel_id=1, source_target_pairs={{0,1},{1,2},{2,3},{3,0},{4,5},{5,6},{6,7},{7,4},{8,9},{9,10},{10,1... | collective-permute-start | bytes 1572872 | tf_op jit(solution)/shard_map/ppermute | solution.py:354
  13.1 18.0 %collective-permute-start.10 = (bf16[2,8,64,256]{3,2,1,0:T(8,128)(2,1)}, bf16[2,8,64,256]{3,2,1,0:T(8,128)(2,1)S(1)}, u32[]{:S(2)}, u32[]{:S(2)}) collective-permute-start(bf16[2,8,64,256]{3,2,1,0:T(8,128)(2,1)} %get-tuple-element.26.refs_0_), channel_id=1, source_target_pairs={{0,3},{1,0},{2,1},{3,2},{4,7},{5,4},{6,5},{7,6},{8,11},{9,8},{10,9... | collective-permute-start | bytes 1572872 | tf_op jit(solution)/shard_map/ppermute | solution.py:354
  16.3 4.3 %copy-start.24 = (bf16[4,64,256]{2,1,0:T(8,128)(2,1)}, bf16[4,64,256]{2,1,0:T(8,128)(2,1)S(1)}, u32[]{:S(2)}) copy-start(bf16[4,64,256]{2,1,0:T(8,128)(2,1)S(1)} %collective-permute-done.2.low_ref) | copy-start | bytes 393220
  17.4 3.2 %copy-start.25 = (bf16[4,64,256]{2,1,0:T(8,128)(2,1)}, bf16[4,64,256]{2,1,0:T(8,128)(2,1)S(1)}, u32[]{:S(2)}) copy-start(bf16[4,64,256]{2,1,0:T(8,128)(2,1)S(1)} %collective-permute-done.3.high_ref) | copy-start | bytes 393220
  17.4 20.9 %collective-permute-start.7 = (bf16[2,8,64,256]{3,2,1,0:T(8,128)(2,1)}, bf16[2,8,64,256]{3,2,1,0:T(8,128)(2,1)S(1)}, u32[]{:S(2)}, u32[]{:S(2)}) collective-permute-start(bf16[2,8,64,256]{3,2,1,0:T(8,128)(2,1)} %get-tuple-element.35.refs_4_.refs_0_), channel_id=1, source_target_pairs={{0,1},{1,2},{2,3},{3,0},{4,5},{5,6},{6,7},{7,4},{8,9},{9,10},{10,1... | collective-permute-start | bytes 1572872 | tf_op jit(solution)/shard_map/ppermute | solution.py:354
  18.6 19.6 %collective-permute-start.8 = (bf16[2,8,64,256]{3,2,1,0:T(8,128)(2,1)}, bf16[2,8,64,256]{3,2,1,0:T(8,128)(2,1)S(1)}, u32[]{:S(2)}, u32[]{:S(2)}) collective-permute-start(bf16[2,8,64,256]{3,2,1,0:T(8,128)(2,1)} %get-tuple-element.35.refs_4_.refs_0_), channel_id=1, source_target_pairs={{0,3},{1,0},{2,1},{3,2},{4,7},{5,4},{6,5},{7,6},{8,11},{9,8},{10,9... | collective-permute-start | bytes 1572872 | tf_op jit(solution)/shard_map/ppermute | solution.py:354
  23.7 27.2 %copy-start.6 = (bf16[2,8,64,256]{3,2,1,0:T(8,128)(2,1)S(1)}, bf16[2,8,64,256]{3,2,1,0:T(8,128)(2,1)}, u32[]{:S(2)}) copy-start(bf16[2,8,64,256]{3,2,1,0:T(8,128)(2,1)} %get-tuple-element.38.refs_8_.refs_4_) | copy-start | bytes 1572868
  23.7 17.8 %collective-permute-start.4 = (bf16[528,256]{1,0:T(8,128)(2,1)}, bf16[528,256]{1,0:T(8,128)(2,1)S(1)}, u32[]{:S(2)}, u32[]{:S(2)}) collective-permute-start(bf16[528,256]{1,0:T(8,128)(2,1)} %get-tuple-element.32.refs_8_.refs_12_), channel_id=1, source_target_pairs={{0,8},{4,12},{8,16},{12,20},{16,24},{20,28},{24,32},{28,36},{32,40... | collective-permute-start | bytes 811016 | tf_op jit(solution)/shard_map/ppermute | solution.py:359
  29.1 25.5 %copy-start.10 = (bf16[2,8,64,256]{3,2,1,0:T(8,128)(2,1)}, bf16[2,8,64,256]{3,2,1,0:T(8,128)(2,1)S(1)}, u32[]{:S(2)}) copy-start(bf16[2,8,64,256]{3,2,1,0:T(8,128)(2,1)S(1)} %collective-permute-done.9.refs_1_) | copy-start | bytes 1572868
  29.1 12.4 %collective-permute-start.5 = (bf16[528,256]{1,0:T(8,128)(2,1)}, bf16[528,256]{1,0:T(8,128)(2,1)S(1)}, u32[]{:S(2)}, u32[]{:S(2)}) collective-permute-start(bf16[528,256]{1,0:T(8,128)(2,1)} %get-tuple-element.32.refs_8_.refs_12_), channel_id=1, source_target_pairs={{0,4},{4,16},{8,12},{12,24},{16,20},{20,32},{24,28},{28,40},{32,36... | collective-permute-start | bytes 811016 | tf_op jit(solution)/shard_map/ppermute | solution.py:376
  31.0 7.2 %copy-start.11 = (bf16[2,8,64,256]{3,2,1,0:T(8,128)(2,1)}, bf16[2,8,64,256]{3,2,1,0:T(8,128)(2,1)S(1)}, u32[]{:S(2)}) copy-start(bf16[2,8,64,256]{3,2,1,0:T(8,128)(2,1)S(1)} %collective-permute-done.10.refs_2_) | copy-start | bytes 1572868
  31.1 18.4 %collective-permute-start.12 = (bf16[2,8,64,256]{3,2,1,0:T(8,128)(2,1)S(1)}, bf16[2,8,64,256]{3,2,1,0:T(8,128)(2,1)}, u32[]{:S(2)}, u32[]{:S(2)}) collective-permute-start(bf16[2,8,64,256]{3,2,1,0:T(8,128)(2,1)S(1)} %collective-permute-done.9.refs_1_), channel_id=1, source_target_pairs={{0,1},{1,2},{2,3},{3,0},{4,5},{5,6},{6,7},{7,4},{8,9},{9,10},{10,1... | collective-permute-start | bytes 1572872 | tf_op jit(solution)/shard_map/ppermute | solution.py:354
  38.3 16.4 %copy-start = (bf16[2,8,64,256]{3,2,1,0:T(8,128)(2,1)}, bf16[2,8,64,256]{3,2,1,0:T(8,128)(2,1)S(1)}, u32[]{:S(2)}) copy-start(bf16[2,8,64,256]{3,2,1,0:T(8,128)(2,1)S(1)} %collective-permute-done.7.refs_5_.refs_1_) | copy-start | bytes 1572868
  38.3 16.4 %copy-start.1 = (bf16[2,8,64,256]{3,2,1,0:T(8,128)(2,1)}, bf16[2,8,64,256]{3,2,1,0:T(8,128)(2,1)S(1)}, u32[]{:S(2)}) copy-start(bf16[2,8,64,256]{3,2,1,0:T(8,128)(2,1)S(1)} %collective-permute-done.8.refs_6_.refs_2_) | copy-start | bytes 1572868
  38.3 12.6 %collective-permute-start.11 = (bf16[2,8,64,256]{3,2,1,0:T(8,128)(2,1)S(1)}, bf16[2,8,64,256]{3,2,1,0:T(8,128)(2,1)S(1)}, u32[]{:S(2)}, u32[]{:S(2)}) collective-permute-start(bf16[2,8,64,256]{3,2,1,0:T(8,128)(2,1)S(1)} %collective-permute-done.8.refs_6_.refs_2_), channel_id=1, source_target_pairs={{0,3},{1,0},{2,1},{3,2},{4,7},{5,4},{6,5},{7,6},{8,11},{9,8},{10,9... | collective-permute-start | bytes 1572872 | tf_op jit(solution)/shard_map/ppermute | solution.py:354
  41.5 1.7 %copy-start.3 = (bf16[528,256]{1,0:T(8,128)(2,1)}, bf16[528,256]{1,0:T(8,128)(2,1)S(1)}, u32[]{:S(2)}) copy-start(bf16[528,256]{1,0:T(8,128)(2,1)S(1)} %collective-permute-done.4.two_ref.refs_10_.refs_14_) | copy-start | bytes 811012
  41.5 1.7 %copy-start.4 = (bf16[528,256]{1,0:T(8,128)(2,1)}, bf16[528,256]{1,0:T(8,128)(2,1)S(1)}, u32[]{:S(2)}) copy-start(bf16[528,256]{1,0:T(8,128)(2,1)S(1)} %collective-permute-done.5.three_ref.refs_11_.refs_15_) | copy-start | bytes 811012
  41.5 1.6 %collective-permute-start.6 = (bf16[528,256]{1,0:T(8,128)(2,1)S(1)}, bf16[528,256]{1,0:T(8,128)(2,1)S(1)}, u32[]{:S(2)}, u32[]{:S(2)}) collective-permute-start(bf16[528,256]{1,0:T(8,128)(2,1)S(1)} %collective-permute-done.4.two_ref.refs_10_.refs_14_), channel_id=1, source_target_pairs={{0,4},{4,0},{8,12},{12,8},{16,20},{20,16},{24,28},{28,24},{32,36},... | collective-permute-start | bytes 811016 | tf_op jit(solution)/shard_map/ppermute | solution.py:379
  50.8 3.8 %copy-start.2 = (bf16[2,8,64,256]{3,2,1,0:T(8,128)(2,1)}, bf16[2,8,64,256]{3,2,1,0:T(8,128)(2,1)S(1)}, u32[]{:S(2)}) copy-start(bf16[2,8,64,256]{3,2,1,0:T(8,128)(2,1)S(1)} %collective-permute-done.11.refs_7_.refs_3_) | copy-start | bytes 1572868
  50.8 13.9 %collective-permute-start.13 = (bf16[2,8,64,256]{3,2,1,0:T(8,128)(2,1)S(1)}, bf16[2,8,64,256]{3,2,1,0:T(8,128)(2,1)S(1)}, u32[]{:S(2)}, u32[]{:S(2)}) collective-permute-start(bf16[2,8,64,256]{3,2,1,0:T(8,128)(2,1)S(1)} %copy-done.6), channel_id=1, source_target_pairs={{0,1},{1,2},{2,3},{3,0},{4,5},{5,6},{6,7},{7,4},{8,9},{9,10},{10,1... | collective-permute-start | bytes 1572872 | tf_op jit(solution)/shard_map/ppermute | solution.py:354
  50.8 28.6 %collective-permute-start.14 = (bf16[2,8,64,256]{3,2,1,0:T(8,128)(2,1)S(1)}, bf16[2,8,64,256]{3,2,1,0:T(8,128)(2,1)S(1)}, u32[]{:S(2)}, u32[]{:S(2)}) collective-permute-start(bf16[2,8,64,256]{3,2,1,0:T(8,128)(2,1)S(1)} %copy-done.6), channel_id=1, source_target_pairs={{0,3},{1,0},{2,1},{3,2},{4,7},{5,4},{6,5},{7,6},{8,11},{9,8},{10,9... | collective-permute-start | bytes 1572872 | tf_op jit(solution)/shard_map/ppermute | solution.py:354
  54.6 24.8 %copy-start.17 = (bf16[1,8,64,256]{3,2,1,0:T(8,128)(2,1)S(1)}, bf16[1,8,64,256]{3,2,1,0:T(8,128)(2,1)}, u32[]{:S(2)}) copy-start(bf16[1,8,64,256]{3,2,1,0:T(8,128)(2,1)} %get-tuple-element.39.refs_8_) | copy-start | bytes 786436
  59.0 20.3 %collective-permute-start.19 = (bf16[512,256]{1,0:T(8,128)(2,1)}, bf16[512,256]{1,0:T(8,128)(2,1)S(1)}, u32[]{:S(2)}, u32[]{:S(2)}) collective-permute-start(bf16[512,256]{1,0:T(8,128)(2,1)} %get-tuple-element.41.refs_16_), channel_id=1, source_target_pairs={{0,8},{4,12},{8,16},{12,20},{16,24},{20,28},{24,32},{28,36},{32,40... | collective-permute-start | bytes 786440 | tf_op jit(solution)/shard_map/ppermute | solution.py:359
  62.8 16.5 %collective-permute-start.20 = (bf16[512,256]{1,0:T(8,128)(2,1)}, bf16[512,256]{1,0:T(8,128)(2,1)S(1)}, u32[]{:S(2)}, u32[]{:S(2)}) collective-permute-start(bf16[512,256]{1,0:T(8,128)(2,1)} %get-tuple-element.41.refs_16_), channel_id=1, source_target_pairs={{0,4},{4,16},{8,12},{12,24},{16,20},{20,32},{24,28},{28,40},{32,36... | collective-permute-start | bytes 786440 | tf_op jit(solution)/shard_map/ppermute | solution.py:376
  64.8 16.7 %copy-start.7 = (bf16[2,8,64,256]{3,2,1,0:T(8,128)(2,1)}, bf16[2,8,64,256]{3,2,1,0:T(8,128)(2,1)S(1)}, u32[]{:S(2)}) copy-start(bf16[2,8,64,256]{3,2,1,0:T(8,128)(2,1)S(1)} %collective-permute-done.13.refs_9_.refs_5_) | copy-start | bytes 1572868
  64.8 16.7 %collective-permute-start.15 = (bf16[2,8,64,256]{3,2,1,0:T(8,128)(2,1)S(1)}, bf16[2,8,64,256]{3,2,1,0:T(8,128)(2,1)S(1)}, u32[]{:S(2)}, u32[]{:S(2)}) collective-permute-start(bf16[2,8,64,256]{3,2,1,0:T(8,128)(2,1)S(1)} %collective-permute-done.13.refs_9_.refs_5_), channel_id=1, source_target_pairs={{0,1},{1,2},{2,3},{3,0},{4,5},{5,6},{6,7},{7,4},{8,9},{9,10},{10,1... | collective-permute-start | bytes 1572872 | tf_op jit(solution)/shard_map/ppermute | solution.py:354
  79.3 2.2 %copy-start.12 = (bf16[512,256]{1,0:T(8,128)(2,1)}, bf16[512,256]{1,0:T(8,128)(2,1)S(1)}, u32[]{:S(2)}) copy-start(bf16[512,256]{1,0:T(8,128)(2,1)S(1)} %collective-permute-done.19.refs_18_) | copy-start | bytes 786436
  79.3 2.2 %copy-start.13 = (bf16[512,256]{1,0:T(8,128)(2,1)}, bf16[512,256]{1,0:T(8,128)(2,1)S(1)}, u32[]{:S(2)}) copy-start(bf16[512,256]{1,0:T(8,128)(2,1)S(1)} %collective-permute-done.20.refs_19_) | copy-start | bytes 786436
  79.3 2.1 %collective-permute-start.21 = (bf16[512,256]{1,0:T(8,128)(2,1)S(1)}, bf16[512,256]{1,0:T(8,128)(2,1)S(1)}, u32[]{:S(2)}, u32[]{:S(2)}) collective-permute-start(bf16[512,256]{1,0:T(8,128)(2,1)S(1)} %collective-permute-done.19.refs_18_), channel_id=1, source_target_pairs={{0,4},{4,0},{8,12},{12,8},{16,20},{20,16},{24,28},{28,24},{32,36},... | collective-permute-start | bytes 786440 | tf_op jit(solution)/shard_map/ppermute | solution.py:379
  79.4 2.1 %copy-start.8 = (bf16[2,8,64,256]{3,2,1,0:T(8,128)(2,1)}, bf16[2,8,64,256]{3,2,1,0:T(8,128)(2,1)S(1)}, u32[]{:S(2)}) copy-start(bf16[2,8,64,256]{3,2,1,0:T(8,128)(2,1)S(1)} %collective-permute-done.14.refs_10_.refs_6_) | copy-start | bytes 1572868
  79.4 12.8 %collective-permute-start.17 = (bf16[1,8,64,256]{3,2,1,0:T(8,128)(2,1)S(1)}, bf16[1,8,64,256]{3,2,1,0:T(8,128)(2,1)S(1)}, u32[]{:S(2)}, u32[]{:S(2)}) collective-permute-start(bf16[1,8,64,256]{3,2,1,0:T(8,128)(2,1)S(1)} %copy-done.17), channel_id=1, source_target_pairs={{0,3},{1,0},{2,1},{3,2},{4,7},{5,4},{6,5},{7,6},{8,11},{9,8},{10,9... | collective-permute-start | bytes 786440 | tf_op jit(solution)/shard_map/ppermute | solution.py:354
  81.5 0.9 copy-start.9
  87.8 12.5 %collective-permute-start.22 = (bf16[512,256]{1,0:T(8,128)(2,1)}, bf16[512,256]{1,0:T(8,128)(2,1)S(1)}, u32[]{:S(2)}, u32[]{:S(2)}) collective-permute-start(bf16[512,256]{1,0:T(8,128)(2,1)} %get-tuple-element.44.refs_20_), channel_id=1, source_target_pairs={{0,8},{4,12},{8,16},{12,20},{16,24},{20,28},{24,32},{28,36},{32,40... | collective-permute-start | bytes 786440 | tf_op jit(solution)/shard_map/ppermute | solution.py:359
  90.2 15.4 %collective-permute-start.23 = (bf16[512,256]{1,0:T(8,128)(2,1)}, bf16[512,256]{1,0:T(8,128)(2,1)S(1)}, u32[]{:S(2)}, u32[]{:S(2)}) collective-permute-start(bf16[512,256]{1,0:T(8,128)(2,1)} %get-tuple-element.44.refs_20_), channel_id=1, source_target_pairs={{0,4},{4,16},{8,12},{12,24},{16,20},{20,32},{24,28},{28,40},{32,36... | collective-permute-start | bytes 786440 | tf_op jit(solution)/shard_map/ppermute | solution.py:376
  92.1 13.5 %collective-permute-start.16 = (bf16[1,8,64,256]{3,2,1,0:T(8,128)(2,1)S(1)}, bf16[1,8,64,256]{3,2,1,0:T(8,128)(2,1)S(1)}, u32[]{:S(2)}, u32[]{:S(2)}) collective-permute-start(bf16[1,8,64,256]{3,2,1,0:T(8,128)(2,1)S(1)} %copy-done.17), channel_id=1, source_target_pairs={{0,1},{1,2},{2,3},{3,0},{4,5},{5,6},{6,7},{7,4},{8,9},{9,10},{10,1... | collective-permute-start | bytes 786440 | tf_op jit(solution)/shard_map/ppermute | solution.py:354
  92.3 14.9 %copy-start.18 = (bf16[1,8,64,256]{3,2,1,0:T(8,128)(2,1)}, bf16[1,8,64,256]{3,2,1,0:T(8,128)(2,1)S(1)}, u32[]{:S(2)}) copy-start(bf16[1,8,64,256]{3,2,1,0:T(8,128)(2,1)S(1)} %collective-permute-done.17.refs_10_) | copy-start | bytes 786436
  92.3 13.3 %collective-permute-start.18 = (bf16[1,8,64,256]{3,2,1,0:T(8,128)(2,1)S(1)}, bf16[1,8,64,256]{3,2,1,0:T(8,128)(2,1)S(1)}, u32[]{:S(2)}, u32[]{:S(2)}) collective-permute-start(bf16[1,8,64,256]{3,2,1,0:T(8,128)(2,1)S(1)} %collective-permute-done.17.refs_10_), channel_id=1, source_target_pairs={{0,3},{1,0},{2,1},{3,2},{4,7},{5,4},{6,5},{7,6},{8,11},{9,8},{10,9... | collective-permute-start | bytes 786440 | tf_op jit(solution)/shard_map/ppermute | solution.py:354
  100.3 6.8 %copy-start.19 = (bf16[512,256]{1,0:T(8,128)(2,1)}, bf16[512,256]{1,0:T(8,128)(2,1)S(1)}, u32[]{:S(2)}) copy-start(bf16[512,256]{1,0:T(8,128)(2,1)S(1)} %collective-permute-done.22.refs_22_) | copy-start | bytes 786436
  105.6 1.5 %copy-start.20 = (bf16[512,256]{1,0:T(8,128)(2,1)}, bf16[512,256]{1,0:T(8,128)(2,1)S(1)}, u32[]{:S(2)}) copy-start(bf16[512,256]{1,0:T(8,128)(2,1)S(1)} %collective-permute-done.23.refs_23_) | copy-start | bytes 786436
  105.6 1.5 %collective-permute-start.24 = (bf16[512,256]{1,0:T(8,128)(2,1)S(1)}, bf16[512,256]{1,0:T(8,128)(2,1)S(1)}, u32[]{:S(2)}, u32[]{:S(2)}) collective-permute-start(bf16[512,256]{1,0:T(8,128)(2,1)S(1)} %collective-permute-done.22.refs_22_), channel_id=1, source_target_pairs={{0,4},{4,0},{8,12},{12,8},{16,20},{20,16},{24,28},{28,24},{32,36},... | collective-permute-start | bytes 786440 | tf_op jit(solution)/shard_map/ppermute | solution.py:379
  105.6 1.5 %copy-start.21 = (bf16[1,8,64,256]{3,2,1,0:T(8,128)(2,1)}, bf16[1,8,64,256]{3,2,1,0:T(8,128)(2,1)S(1)}, u32[]{:S(2)}) copy-start(bf16[1,8,64,256]{3,2,1,0:T(8,128)(2,1)S(1)} %collective-permute-done.16.refs_9_) | copy-start | bytes 786436
  105.6 1.5 %copy-start.22 = (bf16[1,8,64,256]{3,2,1,0:T(8,128)(2,1)}, bf16[1,8,64,256]{3,2,1,0:T(8,128)(2,1)S(1)}, u32[]{:S(2)}) copy-start(bf16[1,8,64,256]{3,2,1,0:T(8,128)(2,1)S(1)} %collective-permute-done.18.refs_11_) | copy-start | bytes 786436
  (3 other events, 2.1 us)
where the time goes:
time: 117 us; the launch traced here: 115 us
  waiting for transfers between devices  44.4 us (38%)
  starting transfers between devices  41.7 us (36%)
  Pallas kernels  26.4 us (23%)
  local copies, waits for them, and re-layouts  2.35 us (2%)
    ppermute x16, starting transfers between devices, round_x(): lax.ppermute(block, 'rhs', [(i, (i + distance) % size) for i in range(siz...  25.5 us
    ppermute x3, waiting for transfers between devices, up(): lax.ppermute(block, 'rows', [(i, i + distance) for i in range(size - dist...  19.3 us
    pallas_call x3, Pallas kernels, level_call(): pl.pallas_call(functools.partial(level_kernel, level, used), out_shape=[j...  17.2 us
    ppermute x16, waiting for transfers between devices, round_x(): lax.ppermute(block, 'rhs', [(i, (i + distance) % size) for i in range(siz...  16.8 us
    ppermute x3, starting transfers between devices, up(): lax.ppermute(block, 'rows', [(i, i + distance) for i in range(size - dist...  10.2 us
    ppermute x3, starting transfers between devices, shift(): lax.ppermute(solved, 'rows', [(i, i + (3 if i % 2 else 1)) for i in range...  5.75 us
    ppermute x3, waiting for transfers between devices, shift(): lax.ppermute(solved, 'rows', [(i, i + (3 if i % 2 else 1)) for i in range...  5.29 us
    pallas_call x1, Pallas kernels, sort_call(): pl.pallas_call(sort_kernel, out_shape=[jax.ShapeDtypeStruct((high - low,)...  3.42 us
  transfers between devices with their start and end apart: 25, of which 12 were waited for; matrix products, arithmetic and copies ran while one was open for 0% of the time, Pallas kernels for 16%

commit v1 on v0

--- a/solution.py
+++ b/solution.py
@@ -13,7 +13,7 @@
 ANY = pl.BlockSpec(memory_space=pl.ANY)
 SMEM = pl.BlockSpec(memory_space=pltpu.SMEM)
 VMEM = pl.BlockSpec(memory_space=pltpu.VMEM)
-PARAMS = pltpu.CompilerParams(vmem_limit_bytes=58 * 2**20)
+PARAMS = pltpu.CompilerParams(vmem_limit_bytes=61 * 2**20)
 
 PLACES = {1: range(0, 4), 2: range(1, 6), 3: range(2, 7), 0: range(4, 8)}
 CHUNKS = ((0, 2), (2, 4), (4, 6), (6, 7))

time: 117 us -> 117 us (level)
  the two profiles are of different devices: /device:TPU:8 before, /device:TPU:1 now
where the time goes in v1:
time: 117 us
  starting transfers between devices  65.5 us (56%)
  Pallas kernels  25.6 us (22%)
  waiting for transfers between devices  23.2 us (20%)
  local copies, waits for them, and re-layouts  2.31 us (2%)
    ppermute x3, starting transfers between devices, shift(): lax.ppermute(solved, 'rows', [(i, i + (3 if i % 2 else 1)) for i in range...  26.3 us
    ppermute x16, starting transfers between devices, round_x(): lax.ppermute(block, 'rhs', [(i, (i + distance) % size) for i in range(siz...  22 us
    pallas_call x3, Pallas kernels, level_call(): pl.pallas_call(functools.partial(level_kernel, level, used), out_shape=[j...  16.3 us
    ppermute x3, starting transfers between devices, up(): lax.ppermute(block, 'rows', [(i, i + distance) for i in range(size - dist...  14.2 us
    ppermute x16, waiting for transfers between devices, round_x(): lax.ppermute(block, 'rhs', [(i, (i + distance) % size) for i in range(siz...  13.8 us
    ppermute x3, waiting for transfers between devices, shift(): lax.ppermute(solved, 'rows', [(i, i + (3 if i % 2 else 1)) for i in range...  7.68 us
    pallas_call x1, Pallas kernels, sort_call(): pl.pallas_call(sort_kernel, out_shape=[jax.ShapeDtypeStruct((high - low,)...  3.44 us
    pallas_call x1, Pallas kernels, first_call(): pl.pallas_call(first_kernel, out_shape=[jax.ShapeDtypeStruct(right.shape,...  3.13 us
  transfers between devices with their start and end apart: 25, of which 11 were waited for; matrix products, arithmetic and copies ran while one was open for 0% of the time, Pallas kernels for 16%

profile of v1, /device:TPU:1, one launch (start us, length us, event | category | flops | bytes accessed | tf_op | source)
XLA Modules:
  0.0 117.1 jit_solution(10726278770570900275)
XLA Ops:
  0.0 2.0 %collective-permute-start = (bf16[8,64,256]{2,1,0:T(8,128)(2,1)}, bf16[8,64,256]{2,1,0:T(8,128)(2,1)S(1)}, u32[]{:S(2)}, u32[]{:S(2)}) collective-permute-start(bf16[8,64,256]{2,1,0:T(8,128)(2,1)} %own_ref.1), channel_id=1, source_target_pairs={{0,1},{1,2},{2,3},{3,0},{4,5},{5,6},{6,7},{7,4},{8,9},{9,10},{10,1... | collective-permute-start | bytes 786440 | tf_op jit(solution)/shard_map/ppermute | solution.py:354
  2.0 1.3 %collective-permute-start.1 = (bf16[8,64,256]{2,1,0:T(8,128)(2,1)}, bf16[8,64,256]{2,1,0:T(8,128)(2,1)S(1)}, u32[]{:S(2)}, u32[]{:S(2)}) collective-permute-start(bf16[8,64,256]{2,1,0:T(8,128)(2,1)} %own_ref.1), channel_id=1, source_target_pairs={{0,3},{1,0},{2,1},{3,2},{4,7},{5,4},{6,5},{7,6},{8,11},{9,8},{10,9... | collective-permute-start | bytes 786440 | tf_op jit(solution)/shard_map/ppermute | solution.py:354
  3.3 3.4 %shard_map.55 = (bf16[2,8,64,256]{3,2,1,0:T(8,128)(2,1)}, bf16[2,8,64,256]{3,2,1,0:T(8,128)(2,1)}, bf16[2,8,64,256]{3,2,1,0:T(8,128)(2,1)}, bf16[1,8,64,256]{3,2,1,0:T(8,128)(2,1)}) custom-call(s32[8]{0:T(128)} %level_ref.5, bf16[8,8,64,256]{3,2,1,0:T(8,128)(2,1)} %off_ref.1), custom_call_target="tpu_custom_call" | custom-call | tf_op jit(solution)/shard_map/pallas_call | solution.py:55
  6.8 0.5 collective-permute-done.before_ref
  7.3 1.6 %collective-permute-done.1.after_ref = bf16[8,64,256]{2,1,0:T(8,128)(2,1)S(1)} collective-permute-done((bf16[8,64,256]{2,1,0:T(8,128)(2,1)}, bf16[8,64,256]{2,1,0:T(8,128)(2,1)S(1)}, u32[]{:S(2)}, u32[]{:S(2)}) %collective-permute-start.1) | collective-permute-done | bytes 262176 | tf_op jit(solution)/shard_map/ppermute | solution.py:354
  8.9 1.6 %collective-permute-start.2 = (bf16[4,64,256]{2,1,0:T(8,128)(2,1)S(1)}, bf16[4,64,256]{2,1,0:T(8,128)(2,1)S(1)}, u32[]{:S(2)}, u32[]{:S(2)}) collective-permute-start(bf16[4,64,256]{2,1,0:T(8,128)(2,1)S(1)} %slice.8), channel_id=1, source_target_pairs={{0,1},{1,2},{2,3},{3,0},{4,5},{5,6},{6,7},{7,4},{8,9},{9,10},{10,1... | collective-permute-start | bytes 393224 | tf_op jit(solution)/shard_map/ppermute | solution.py:354
  10.4 1.2 %collective-permute-start.3 = (bf16[4,64,256]{2,1,0:T(8,128)(2,1)S(1)}, bf16[4,64,256]{2,1,0:T(8,128)(2,1)S(1)}, u32[]{:S(2)}, u32[]{:S(2)}) collective-permute-start(bf16[4,64,256]{2,1,0:T(8,128)(2,1)S(1)} %slice.9), channel_id=1, source_target_pairs={{0,3},{1,0},{2,1},{3,2},{4,7},{5,4},{6,5},{7,6},{8,11},{9,8},{10,9... | collective-permute-start | bytes 393224 | tf_op jit(solution)/shard_map/ppermute | solution.py:354
  11.6 0.3 collective-permute-start.9
  11.9 2.4 %collective-permute-start.10 = (bf16[2,8,64,256]{3,2,1,0:T(8,128)(2,1)}, bf16[2,8,64,256]{3,2,1,0:T(8,128)(2,1)S(1)}, u32[]{:S(2)}, u32[]{:S(2)}) collective-permute-start(bf16[2,8,64,256]{3,2,1,0:T(8,128)(2,1)} %get-tuple-element.26.refs_0_), channel_id=1, source_target_pairs={{0,3},{1,0},{2,1},{3,2},{4,7},{5,4},{6,5},{7,6},{8,11},{9,8},{10,9... | collective-permute-start | bytes 1572872 | tf_op jit(solution)/shard_map/ppermute | solution.py:354
  14.3 0.6 collective-permute-start.7
  14.9 2.2 %collective-permute-start.8 = (bf16[2,8,64,256]{3,2,1,0:T(8,128)(2,1)}, bf16[2,8,64,256]{3,2,1,0:T(8,128)(2,1)S(1)}, u32[]{:S(2)}, u32[]{:S(2)}) collective-permute-start(bf16[2,8,64,256]{3,2,1,0:T(8,128)(2,1)} %get-tuple-element.35.refs_4_.refs_0_), channel_id=1, source_target_pairs={{0,3},{1,0},{2,1},{3,2},{4,7},{5,4},{6,5},{7,6},{8,11},{9,8},{10,9... | collective-permute-start | bytes 1572872 | tf_op jit(solution)/shard_map/ppermute | solution.py:354
  17.1 3.1 %shard_map.56 = (bf16[8,128,256]{2,1,0:T(8,128)(2,1)}, bf16[8,256,256]{2,1,0:T(8,128)(2,1)}, bf16[528,256]{1,0:T(8,128)(2,1)}) custom-call(s32[1]{0:T(128)} %bitcast.1.x_ref, s32[8]{0:T(128)} %level_ref.5, bf16[8,128,256]{2,1,0:T(8,128)(2,1)} %right_ref.7, bf16[8,64,256]{2,1,0:T(8,128)(2,1)} %own_ref.1, bf16[8,64,256]{2,1,0:T(8,128)(2,1)} %copy-done.13, ...), custom_call_target="tpu_custom_call" | custom-call | flops 67108864 | bytes 3145728 | tf_op jit(solution)/shard_map/pallas_call | solution.py:195
  20.2 4.2 %collective-permute-start.4 = (bf16[528,256]{1,0:T(8,128)(2,1)}, bf16[528,256]{1,0:T(8,128)(2,1)S(1)}, u32[]{:S(2)}, u32[]{:S(2)}) collective-permute-start(bf16[528,256]{1,0:T(8,128)(2,1)} %get-tuple-element.32.refs_8_.refs_12_), channel_id=1, source_target_pairs={{0,8},{4,12},{8,16},{12,20},{16,24},{20,28},{24,32},{28,36},{32,40... | collective-permute-start | bytes 811016 | tf_op jit(solution)/shard_map/ppermute | solution.py:359
  24.5 1.7 %collective-permute-done.9.refs_1_ = bf16[2,8,64,256]{3,2,1,0:T(8,128)(2,1)} collective-permute-done((bf16[2,8,64,256]{3,2,1,0:T(8,128)(2,1)}, bf16[2,8,64,256]{3,2,1,0:T(8,128)(2,1)}, u32[]{:S(2)}, u32[]{:S(2)}) %collective-permute-start.9) | collective-permute-done | bytes 524320 | tf_op jit(solution)/shard_map/ppermute | solution.py:354
  26.1 9.4 %collective-permute-start.5 = (bf16[528,256]{1,0:T(8,128)(2,1)}, bf16[528,256]{1,0:T(8,128)(2,1)S(1)}, u32[]{:S(2)}, u32[]{:S(2)}) collective-permute-start(bf16[528,256]{1,0:T(8,128)(2,1)} %get-tuple-element.32.refs_8_.refs_12_), channel_id=1, source_target_pairs={{0,4},{4,16},{8,12},{12,24},{16,20},{20,32},{24,28},{28,40},{32,36... | collective-permute-start | bytes 811016 | tf_op jit(solution)/shard_map/ppermute | solution.py:376
  35.5 0.1 collective-permute-start.12
  35.6 1.6 %collective-permute-done.7.refs_5_.refs_1_ = bf16[2,8,64,256]{3,2,1,0:T(8,128)(2,1)S(1)} collective-permute-done((bf16[2,8,64,256]{3,2,1,0:T(8,128)(2,1)}, bf16[2,8,64,256]{3,2,1,0:T(8,128)(2,1)S(1)}, u32[]{:S(2)}, u32[]{:S(2)}) %collective-permute-start.7) | collective-permute-done | bytes 524320 | tf_op jit(solution)/shard_map/ppermute | solution.py:354
  37.3 2.8 %collective-permute-start.11 = (bf16[2,8,64,256]{3,2,1,0:T(8,128)(2,1)S(1)}, bf16[2,8,64,256]{3,2,1,0:T(8,128)(2,1)S(1)}, u32[]{:S(2)}, u32[]{:S(2)}) collective-permute-start(bf16[2,8,64,256]{3,2,1,0:T(8,128)(2,1)S(1)} %collective-permute-done.8.refs_6_.refs_2_), channel_id=1, source_target_pairs={{0,3},{1,0},{2,1},{3,2},{4,7},{5,4},{6,5},{7,6},{8,11},{9,8},{10,9... | collective-permute-start | bytes 1572872 | tf_op jit(solution)/shard_map/ppermute | solution.py:354
  40.1 3.0 %collective-permute-start.6 = (bf16[528,256]{1,0:T(8,128)(2,1)S(1)}, bf16[528,256]{1,0:T(8,128)(2,1)S(1)}, u32[]{:S(2)}, u32[]{:S(2)}) collective-permute-start(bf16[528,256]{1,0:T(8,128)(2,1)S(1)} %collective-permute-done.4.two_ref.refs_10_.refs_14_), channel_id=1, source_target_pairs={{0,4},{4,0},{8,12},{12,8},{16,20},{20,16},{24,28},{28,24},{32,36},... | collective-permute-start | bytes 811016 | tf_op jit(solution)/shard_map/ppermute | solution.py:379
  43.1 1.2 %collective-permute-done.6.one_ref.refs_9_.refs_13_ = bf16[528,256]{1,0:T(8,128)(2,1)S(1)} collective-permute-done((bf16[528,256]{1,0:T(8,128)(2,1)S(1)}, bf16[528,256]{1,0:T(8,128)(2,1)S(1)}, u32[]{:S(2)}, u32[]{:S(2)}) %collective-permute-start.6) | collective-permute-done | bytes 270368 | tf_op jit(solution)/shard_map/ppermute | solution.py:379
  44.3 0.7 copy-done.5
  45.0 2.8 %shard_map.57.table_ref = s32[80]{0:T(128)} custom-call(s32[1]{0:T(128)} %bitcast.rows_at_ref, s32[1]{0:T(128)} %bitcast.1.x_ref, s32[8]{0:T(128)} %level_ref.5, s32[8,8]{1,0:T(8,128)} %columns_ref.1, bf16[528,256]{1,0:T(8,128)(2,1)} %copy-done.5, bf16[528,256]{1,0:T(8,128)(2,1)} %copy-done.3, bf16[528,256]{1,0:T(8,128)(2,1)} %copy-done.4), custom_call_target="tpu_custom_call" | custom-call | flops 1000000000 | bytes 1048576 | tf_op jit(solution)/shard_map/pallas_call | solution.py:105
  47.8 2.7 %collective-permute-done.12.refs_3_ = bf16[2,8,64,256]{3,2,1,0:T(8,128)(2,1)} collective-permute-done((bf16[2,8,64,256]{3,2,1,0:T(8,128)(2,1)}, bf16[2,8,64,256]{3,2,1,0:T(8,128)(2,1)}, u32[]{:S(2)}, u32[]{:S(2)}) %collective-permute-start.12) | collective-permute-done | bytes 524320 | tf_op jit(solution)/shard_map/ppermute | solution.py:354
  50.5 0.0 collective-permute-done.11.refs_7_.refs_3_
  50.5 0.1 collective-permute-start.13
  50.6 2.7 %collective-permute-start.14 = (bf16[2,8,64,256]{3,2,1,0:T(8,128)(2,1)S(1)}, bf16[2,8,64,256]{3,2,1,0:T(8,128)(2,1)}, u32[]{:S(2)}, u32[]{:S(2)}) collective-permute-start(bf16[2,8,64,256]{3,2,1,0:T(8,128)(2,1)S(1)} %copy-done.6), channel_id=1, source_target_pairs={{0,3},{1,0},{2,1},{3,2},{4,7},{5,4},{6,5},{7,6},{8,11},{9,8},{10,9... | collective-permute-start | bytes 1572872 | tf_op jit(solution)/shard_map/ppermute | solution.py:354
  53.2 4.2 %shard_map.58 = (bf16[8,128,256]{2,1,0:T(8,128)(2,1)}, bf16[512,256]{1,0:T(8,128)(2,1)}) custom-call(s32[80]{0:T(128)} %shard_map.57.table_ref, bf16[8,128,256]{2,1,0:T(8,128)(2,1)} %right_ref.7, bf16[8,256,256]{2,1,0:T(8,128)(2,1)} %get-tuple-element.34.diag_ref, ...), custom_call_target="tpu_custom_call", output_to_operand_aliasing={{0}: (15, {})} | custom-call | flops 603979776 | bytes 8388608 | tf_op jit(solution)/shard_map/pallas_call | solution.py:324
  57.4 4.4 %collective-permute-start.19 = (bf16[512,256]{1,0:T(8,128)(2,1)}, bf16[512,256]{1,0:T(8,128)(2,1)S(1)}, u32[]{:S(2)}, u32[]{:S(2)}) collective-permute-start(bf16[512,256]{1,0:T(8,128)(2,1)} %get-tuple-element.41.refs_16_), channel_id=1, source_target_pairs={{0,8},{4,12},{8,16},{12,20},{16,24},{20,28},{24,32},{28,36},{32,40... | collective-permute-start | bytes 786440 | tf_op jit(solution)/shard_map/ppermute | solution.py:359
  61.8 7.8 %collective-permute-start.20 = (bf16[512,256]{1,0:T(8,128)(2,1)}, bf16[512,256]{1,0:T(8,128)(2,1)S(1)}, u32[]{:S(2)}, u32[]{:S(2)}) collective-permute-start(bf16[512,256]{1,0:T(8,128)(2,1)} %get-tuple-element.41.refs_16_), channel_id=1, source_target_pairs={{0,4},{4,16},{8,12},{12,24},{16,20},{20,32},{24,28},{28,40},{32,36... | collective-permute-start | bytes 786440 | tf_op jit(solution)/shard_map/ppermute | solution.py:376
  69.6 0.0 collective-permute-done.13.refs_9_.refs_5_
  69.7 0.1 collective-permute-start.15
  69.7 0.0 collective-permute-done.19.refs_18_
  69.8 4.9 %collective-permute-done.20.refs_19_ = bf16[512,256]{1,0:T(8,128)(2,1)S(1)} collective-permute-done((bf16[512,256]{1,0:T(8,128)(2,1)}, bf16[512,256]{1,0:T(8,128)(2,1)S(1)}, u32[]{:S(2)}, u32[]{:S(2)}) %collective-permute-start.20) | collective-permute-done | bytes 262176 | tf_op jit(solution)/shard_map/ppermute | solution.py:376
  74.7 2.0 %collective-permute-start.17 = (bf16[1,8,64,256]{3,2,1,0:T(8,128)(2,1)}, bf16[1,8,64,256]{3,2,1,0:T(8,128)(2,1)S(1)}, u32[]{:S(2)}, u32[]{:S(2)}) collective-permute-start(bf16[1,8,64,256]{3,2,1,0:T(8,128)(2,1)} %get-tuple-element.39.refs_8_), channel_id=1, source_target_pairs={{0,3},{1,0},{2,1},{3,2},{4,7},{5,4},{6,5},{7,6},{8,11},{9,8},{10,9... | collective-permute-start | bytes 786440 | tf_op jit(solution)/shard_map/ppermute | solution.py:354
  76.7 4.7 %collective-permute-done.15.refs_11_.refs_7_ = bf16[2,8,64,256]{3,2,1,0:T(8,128)(2,1)S(1)} collective-permute-done((bf16[2,8,64,256]{3,2,1,0:T(8,128)(2,1)S(1)}, bf16[2,8,64,256]{3,2,1,0:T(8,128)(2,1)S(1)}, u32[]{:S(2)}, u32[]{:S(2)}) %collective-permute-start.15) | collective-permute-done | bytes 524320 | tf_op jit(solution)/shard_map/ppermute | solution.py:354
  81.5 0.8 copy-done.8
  82.2 4.6 %shard_map.59 = (bf16[8,128,256]{2,1,0:T(8,128)(2,1)}, bf16[512,256]{1,0:T(8,128)(2,1)}) custom-call(s32[80]{0:T(128)} %shard_map.57.table_ref, bf16[8,128,256]{2,1,0:T(8,128)(2,1)} %right_ref.7, bf16[8,256,256]{2,1,0:T(8,128)(2,1)} %get-tuple-element.34.diag_ref, ...), custom_call_target="tpu_custom_call", output_to_operand_aliasing={{0}: (23, {})} | custom-call | flops 603979776 | bytes 8388608 | tf_op jit(solution)/shard_map/pallas_call | solution.py:324
  86.9 5.6 %collective-permute-start.22 = (bf16[512,256]{1,0:T(8,128)(2,1)}, bf16[512,256]{1,0:T(8,128)(2,1)S(1)}, u32[]{:S(2)}, u32[]{:S(2)}) collective-permute-start(bf16[512,256]{1,0:T(8,128)(2,1)} %get-tuple-element.44.refs_20_), channel_id=1, source_target_pairs={{0,8},{4,12},{8,16},{12,20},{16,24},{20,28},{24,32},{28,36},{32,40... | collective-permute-start | bytes 786440 | tf_op jit(solution)/shard_map/ppermute | solution.py:359
  92.5 9.2 %collective-permute-start.23 = (bf16[512,256]{1,0:T(8,128)(2,1)}, bf16[512,256]{1,0:T(8,128)(2,1)S(1)}, u32[]{:S(2)}, u32[]{:S(2)}) collective-permute-start(bf16[512,256]{1,0:T(8,128)(2,1)} %get-tuple-element.44.refs_20_), channel_id=1, source_target_pairs={{0,4},{4,16},{8,12},{12,24},{16,20},{20,32},{24,28},{28,40},{32,36... | collective-permute-start | bytes 786440 | tf_op jit(solution)/shard_map/ppermute | solution.py:376
  101.7 0.1 collective-permute-start.16
  101.8 2.6 %collective-permute-start.18 = (bf16[1,8,64,256]{3,2,1,0:T(8,128)(2,1)S(1)}, bf16[1,8,64,256]{3,2,1,0:T(8,128)(2,1)S(1)}, u32[]{:S(2)}, u32[]{:S(2)}) collective-permute-start(bf16[1,8,64,256]{3,2,1,0:T(8,128)(2,1)S(1)} %collective-permute-done.17.refs_10_), channel_id=1, source_target_pairs={{0,3},{1,0},{2,1},{3,2},{4,7},{5,4},{6,5},{7,6},{8,11},{9,8},{10,9... | collective-permute-start | bytes 786440 | tf_op jit(solution)/shard_map/ppermute | solution.py:354
  104.4 2.8 %collective-permute-done.23.refs_23_ = bf16[512,256]{1,0:T(8,128)(2,1)S(1)} collective-permute-done((bf16[512,256]{1,0:T(8,128)(2,1)}, bf16[512,256]{1,0:T(8,128)(2,1)S(1)}, u32[]{:S(2)}, u32[]{:S(2)}) %collective-permute-start.23) | collective-permute-done | bytes 262176 | tf_op jit(solution)/shard_map/ppermute | solution.py:376
  107.2 1.0 collective-permute-done.16.refs_9_
  108.2 0.5 collective-permute-done.24.refs_21_
  108.8 0.2 copy-done.19
  108.9 0.1 copy-done.20
  109.0 0.5 copy-done.21
  109.5 7.4 %shard_map.60 = bf16[8,128,256]{2,1,0:T(8,128)(2,1)} custom-call(s32[80]{0:T(128)} %shard_map.57.table_ref, bf16[8,128,256]{2,1,0:T(8,128)(2,1)} %right_ref.7, bf16[8,256,256]{2,1,0:T(8,128)(2,1)} %get-tuple-element.34.diag_ref, bf16[2,8,64,256]{3,2,1,0:T(8,128)(2,1)} %get-tuple-element.35.refs_4_.refs_0_, ...), custom_call_target="tpu_custom_call", output_to_operand_aliasing={{}: (27, {})} | custom-call | flops 603979776 | bytes 8388608 | tf_op jit(solution)/shard_map/pallas_call | solution.py:324
  (58 shorter events, 0.1 us)
Async XLA Ops:
  0.0 7.3 %collective-permute-start = (bf16[8,64,256]{2,1,0:T(8,128)(2,1)}, bf16[8,64,256]{2,1,0:T(8,128)(2,1)S(1)}, u32[]{:S(2)}, u32[]{:S(2)}) collective-permute-start(bf16[8,64,256]{2,1,0:T(8,128)(2,1)} %own_ref.1), channel_id=1, source_target_pairs={{0,1},{1,2},{2,3},{3,0},{4,5},{5,6},{6,7},{7,4},{8,9},{9,10},{10,1... | collective-permute-start | bytes 786440 | tf_op jit(solution)/shard_map/ppermute | solution.py:354
  2.0 6.8 %collective-permute-start.1 = (bf16[8,64,256]{2,1,0:T(8,128)(2,1)}, bf16[8,64,256]{2,1,0:T(8,128)(2,1)S(1)}, u32[]{:S(2)}, u32[]{:S(2)}) collective-permute-start(bf16[8,64,256]{2,1,0:T(8,128)(2,1)} %own_ref.1), channel_id=1, source_target_pairs={{0,3},{1,0},{2,1},{3,2},{4,7},{5,4},{6,5},{7,6},{8,11},{9,8},{10,9... | collective-permute-start | bytes 786440 | tf_op jit(solution)/shard_map/ppermute | solution.py:354
  7.3 9.8 %copy-start.13 = (bf16[8,64,256]{2,1,0:T(8,128)(2,1)}, bf16[8,64,256]{2,1,0:T(8,128)(2,1)S(1)}, u32[]{:S(2)}) copy-start(bf16[8,64,256]{2,1,0:T(8,128)(2,1)S(1)} %collective-permute-done.before_ref) | copy-start | bytes 786436
  8.8 8.2 %copy-start.14 = (bf16[8,64,256]{2,1,0:T(8,128)(2,1)}, bf16[8,64,256]{2,1,0:T(8,128)(2,1)S(1)}, u32[]{:S(2)}) copy-start(bf16[8,64,256]{2,1,0:T(8,128)(2,1)S(1)} %collective-permute-done.1.after_ref) | copy-start | bytes 786436
  8.9 5.4 %collective-permute-start.2 = (bf16[4,64,256]{2,1,0:T(8,128)(2,1)S(1)}, bf16[4,64,256]{2,1,0:T(8,128)(2,1)S(1)}, u32[]{:S(2)}, u32[]{:S(2)}) collective-permute-start(bf16[4,64,256]{2,1,0:T(8,128)(2,1)S(1)} %slice.8), channel_id=1, source_target_pairs={{0,1},{1,2},{2,3},{3,0},{4,5},{5,6},{6,7},{7,4},{8,9},{9,10},{10,1... | collective-permute-start | bytes 393224 | tf_op jit(solution)/shard_map/ppermute | solution.py:354
  10.4 3.9 %collective-permute-start.3 = (bf16[4,64,256]{2,1,0:T(8,128)(2,1)S(1)}, bf16[4,64,256]{2,1,0:T(8,128)(2,1)S(1)}, u32[]{:S(2)}, u32[]{:S(2)}) collective-permute-start(bf16[4,64,256]{2,1,0:T(8,128)(2,1)S(1)} %slice.9), channel_id=1, source_target_pairs={{0,3},{1,0},{2,1},{3,2},{4,7},{5,4},{6,5},{7,6},{8,11},{9,8},{10,9... | collective-permute-start | bytes 393224 | tf_op jit(solution)/shard_map/ppermute | solution.py:354
  11.6 14.5 %collective-permute-start.9 = (bf16[2,8,64,256]{3,2,1,0:T(8,128)(2,1)}, bf16[2,8,64,256]{3,2,1,0:T(8,128)(2,1)}, u32[]{:S(2)}, u32[]{:S(2)}) collective-permute-start(bf16[2,8,64,256]{3,2,1,0:T(8,128)(2,1)} %get-tuple-element.26.refs_0_), channel_id=1, source_target_pairs={{0,1},{1,2},{2,3},{3,0},{4,5},{5,6},{6,7},{7,4},{8,9},{9,10},{10,1... | collective-permute-start | bytes 1572872 | tf_op jit(solution)/shard_map/ppermute | solution.py:354
  11.9 23.6 %collective-permute-start.10 = (bf16[2,8,64,256]{3,2,1,0:T(8,128)(2,1)}, bf16[2,8,64,256]{3,2,1,0:T(8,128)(2,1)S(1)}, u32[]{:S(2)}, u32[]{:S(2)}) collective-permute-start(bf16[2,8,64,256]{3,2,1,0:T(8,128)(2,1)} %get-tuple-element.26.refs_0_), channel_id=1, source_target_pairs={{0,3},{1,0},{2,1},{3,2},{4,7},{5,4},{6,5},{7,6},{8,11},{9,8},{10,9... | collective-permute-start | bytes 1572872 | tf_op jit(solution)/shard_map/ppermute | solution.py:354
  14.3 2.8 %copy-start.22 = (bf16[4,64,256]{2,1,0:T(8,128)(2,1)}, bf16[4,64,256]{2,1,0:T(8,128)(2,1)S(1)}, u32[]{:S(2)}) copy-start(bf16[4,64,256]{2,1,0:T(8,128)(2,1)S(1)} %collective-permute-done.2.low_ref) | copy-start | bytes 393220
  14.3 2.8 %copy-start.23 = (bf16[4,64,256]{2,1,0:T(8,128)(2,1)}, bf16[4,64,256]{2,1,0:T(8,128)(2,1)S(1)}, u32[]{:S(2)}) copy-start(bf16[4,64,256]{2,1,0:T(8,128)(2,1)S(1)} %collective-permute-done.3.high_ref) | copy-start | bytes 393220
  14.3 22.9 %collective-permute-start.7 = (bf16[2,8,64,256]{3,2,1,0:T(8,128)(2,1)}, bf16[2,8,64,256]{3,2,1,0:T(8,128)(2,1)S(1)}, u32[]{:S(2)}, u32[]{:S(2)}) collective-permute-start(bf16[2,8,64,256]{3,2,1,0:T(8,128)(2,1)} %get-tuple-element.35.refs_4_.refs_0_), channel_id=1, source_target_pairs={{0,1},{1,2},{2,3},{3,0},{4,5},{5,6},{6,7},{7,4},{8,9},{9,10},{10,1... | collective-permute-start | bytes 1572872 | tf_op jit(solution)/shard_map/ppermute | solution.py:354
  14.9 22.4 %collective-permute-start.8 = (bf16[2,8,64,256]{3,2,1,0:T(8,128)(2,1)}, bf16[2,8,64,256]{3,2,1,0:T(8,128)(2,1)S(1)}, u32[]{:S(2)}, u32[]{:S(2)}) collective-permute-start(bf16[2,8,64,256]{3,2,1,0:T(8,128)(2,1)} %get-tuple-element.35.refs_4_.refs_0_), channel_id=1, source_target_pairs={{0,3},{1,0},{2,1},{3,2},{4,7},{5,4},{6,5},{7,6},{8,11},{9,8},{10,9... | collective-permute-start | bytes 1572872 | tf_op jit(solution)/shard_map/ppermute | solution.py:354
  20.2 30.2 %copy-start.6 = (bf16[2,8,64,256]{3,2,1,0:T(8,128)(2,1)S(1)}, bf16[2,8,64,256]{3,2,1,0:T(8,128)(2,1)}, u32[]{:S(2)}) copy-start(bf16[2,8,64,256]{3,2,1,0:T(8,128)(2,1)} %get-tuple-element.38.refs_8_.refs_4_) | copy-start | bytes 1572868
  20.2 19.8 %collective-permute-start.4 = (bf16[528,256]{1,0:T(8,128)(2,1)}, bf16[528,256]{1,0:T(8,128)(2,1)S(1)}, u32[]{:S(2)}, u32[]{:S(2)}) collective-permute-start(bf16[528,256]{1,0:T(8,128)(2,1)} %get-tuple-element.32.refs_8_.refs_12_), channel_id=1, source_target_pairs={{0,8},{4,12},{8,16},{12,20},{16,24},{20,28},{24,32},{28,36},{32,40... | collective-permute-start | bytes 811016 | tf_op jit(solution)/shard_map/ppermute | solution.py:359
  26.1 13.9 %collective-permute-start.5 = (bf16[528,256]{1,0:T(8,128)(2,1)}, bf16[528,256]{1,0:T(8,128)(2,1)S(1)}, u32[]{:S(2)}, u32[]{:S(2)}) collective-permute-start(bf16[528,256]{1,0:T(8,128)(2,1)} %get-tuple-element.32.refs_8_.refs_12_), channel_id=1, source_target_pairs={{0,4},{4,16},{8,12},{12,24},{16,20},{20,32},{24,28},{28,40},{32,36... | collective-permute-start | bytes 811016 | tf_op jit(solution)/shard_map/ppermute | solution.py:376
  35.5 1.7 %copy-start.9 = (bf16[2,8,64,256]{3,2,1,0:T(8,128)(2,1)}, bf16[2,8,64,256]{3,2,1,0:T(8,128)(2,1)S(1)}, u32[]{:S(2)}) copy-start(bf16[2,8,64,256]{3,2,1,0:T(8,128)(2,1)S(1)} %collective-permute-done.10.refs_2_) | copy-start | bytes 1572868
  35.5 14.9 %collective-permute-start.12 = (bf16[2,8,64,256]{3,2,1,0:T(8,128)(2,1)}, bf16[2,8,64,256]{3,2,1,0:T(8,128)(2,1)}, u32[]{:S(2)}, u32[]{:S(2)}) collective-permute-start(bf16[2,8,64,256]{3,2,1,0:T(8,128)(2,1)} %collective-permute-done.9.refs_1_), channel_id=1, source_target_pairs={{0,1},{1,2},{2,3},{3,0},{4,5},{5,6},{6,7},{7,4},{8,9},{9,10},{10,1... | collective-permute-start | bytes 1572872 | tf_op jit(solution)/shard_map/ppermute | solution.py:354
  37.3 16.0 %copy-start = (bf16[2,8,64,256]{3,2,1,0:T(8,128)(2,1)}, bf16[2,8,64,256]{3,2,1,0:T(8,128)(2,1)S(1)}, u32[]{:S(2)}) copy-start(bf16[2,8,64,256]{3,2,1,0:T(8,128)(2,1)S(1)} %collective-permute-done.7.refs_5_.refs_1_) | copy-start | bytes 1572868
  37.3 16.0 %copy-start.1 = (bf16[2,8,64,256]{3,2,1,0:T(8,128)(2,1)}, bf16[2,8,64,256]{3,2,1,0:T(8,128)(2,1)S(1)}, u32[]{:S(2)}) copy-start(bf16[2,8,64,256]{3,2,1,0:T(8,128)(2,1)S(1)} %collective-permute-done.8.refs_6_.refs_2_) | copy-start | bytes 1572868
  37.3 13.2 %collective-permute-start.11 = (bf16[2,8,64,256]{3,2,1,0:T(8,128)(2,1)S(1)}, bf16[2,8,64,256]{3,2,1,0:T(8,128)(2,1)S(1)}, u32[]{:S(2)}, u32[]{:S(2)}) collective-permute-start(bf16[2,8,64,256]{3,2,1,0:T(8,128)(2,1)S(1)} %collective-permute-done.8.refs_6_.refs_2_), channel_id=1, source_target_pairs={{0,3},{1,0},{2,1},{3,2},{4,7},{5,4},{6,5},{7,6},{8,11},{9,8},{10,9... | collective-permute-start | bytes 1572872 | tf_op jit(solution)/shard_map/ppermute | solution.py:354
  40.1 4.2 %copy-start.3 = (bf16[528,256]{1,0:T(8,128)(2,1)}, bf16[528,256]{1,0:T(8,128)(2,1)S(1)}, u32[]{:S(2)}) copy-start(bf16[528,256]{1,0:T(8,128)(2,1)S(1)} %collective-permute-done.4.two_ref.refs_10_.refs_14_) | copy-start | bytes 811012
  40.1 4.2 %copy-start.4 = (bf16[528,256]{1,0:T(8,128)(2,1)}, bf16[528,256]{1,0:T(8,128)(2,1)S(1)}, u32[]{:S(2)}) copy-start(bf16[528,256]{1,0:T(8,128)(2,1)S(1)} %collective-permute-done.5.three_ref.refs_11_.refs_15_) | copy-start | bytes 811012
  40.1 4.2 %collective-permute-start.6 = (bf16[528,256]{1,0:T(8,128)(2,1)S(1)}, bf16[528,256]{1,0:T(8,128)(2,1)S(1)}, u32[]{:S(2)}, u32[]{:S(2)}) collective-permute-start(bf16[528,256]{1,0:T(8,128)(2,1)S(1)} %collective-permute-done.4.two_ref.refs_10_.refs_14_), channel_id=1, source_target_pairs={{0,4},{4,0},{8,12},{12,8},{16,20},{20,16},{24,28},{28,24},{32,36},... | collective-permute-start | bytes 811016 | tf_op jit(solution)/shard_map/ppermute | solution.py:379
  44.3 0.7 copy-start.5
  50.5 2.8 %copy-start.2 = (bf16[2,8,64,256]{3,2,1,0:T(8,128)(2,1)}, bf16[2,8,64,256]{3,2,1,0:T(8,128)(2,1)S(1)}, u32[]{:S(2)}) copy-start(bf16[2,8,64,256]{3,2,1,0:T(8,128)(2,1)S(1)} %collective-permute-done.11.refs_7_.refs_3_) | copy-start | bytes 1572868
  50.5 19.2 %collective-permute-start.13 = (bf16[2,8,64,256]{3,2,1,0:T(8,128)(2,1)S(1)}, bf16[2,8,64,256]{3,2,1,0:T(8,128)(2,1)S(1)}, u32[]{:S(2)}, u32[]{:S(2)}) collective-permute-start(bf16[2,8,64,256]{3,2,1,0:T(8,128)(2,1)S(1)} %copy-done.6), channel_id=1, source_target_pairs={{0,1},{1,2},{2,3},{3,0},{4,5},{5,6},{6,7},{7,4},{8,9},{9,10},{10,1... | collective-permute-start | bytes 1572872 | tf_op jit(solution)/shard_map/ppermute | solution.py:354
  50.6 24.1 %collective-permute-start.14 = (bf16[2,8,64,256]{3,2,1,0:T(8,128)(2,1)S(1)}, bf16[2,8,64,256]{3,2,1,0:T(8,128)(2,1)}, u32[]{:S(2)}, u32[]{:S(2)}) collective-permute-start(bf16[2,8,64,256]{3,2,1,0:T(8,128)(2,1)S(1)} %copy-done.6), channel_id=1, source_target_pairs={{0,3},{1,0},{2,1},{3,2},{4,7},{5,4},{6,5},{7,6},{8,11},{9,8},{10,9... | collective-permute-start | bytes 1572872 | tf_op jit(solution)/shard_map/ppermute | solution.py:354
  57.4 12.3 %collective-permute-start.19 = (bf16[512,256]{1,0:T(8,128)(2,1)}, bf16[512,256]{1,0:T(8,128)(2,1)S(1)}, u32[]{:S(2)}, u32[]{:S(2)}) collective-permute-start(bf16[512,256]{1,0:T(8,128)(2,1)} %get-tuple-element.41.refs_16_), channel_id=1, source_target_pairs={{0,8},{4,12},{8,16},{12,20},{16,24},{20,28},{24,32},{28,36},{32,40... | collective-permute-start | bytes 786440 | tf_op jit(solution)/shard_map/ppermute | solution.py:359
  61.8 12.8 %collective-permute-start.20 = (bf16[512,256]{1,0:T(8,128)(2,1)}, bf16[512,256]{1,0:T(8,128)(2,1)S(1)}, u32[]{:S(2)}, u32[]{:S(2)}) collective-permute-start(bf16[512,256]{1,0:T(8,128)(2,1)} %get-tuple-element.41.refs_16_), channel_id=1, source_target_pairs={{0,4},{4,16},{8,12},{12,24},{16,20},{20,32},{24,28},{28,40},{32,36... | collective-permute-start | bytes 786440 | tf_op jit(solution)/shard_map/ppermute | solution.py:376
  69.6 11.8 %copy-start.7 = (bf16[2,8,64,256]{3,2,1,0:T(8,128)(2,1)}, bf16[2,8,64,256]{3,2,1,0:T(8,128)(2,1)S(1)}, u32[]{:S(2)}) copy-start(bf16[2,8,64,256]{3,2,1,0:T(8,128)(2,1)S(1)} %collective-permute-done.13.refs_9_.refs_5_) | copy-start | bytes 1572868
  69.7 11.8 %collective-permute-start.15 = (bf16[2,8,64,256]{3,2,1,0:T(8,128)(2,1)S(1)}, bf16[2,8,64,256]{3,2,1,0:T(8,128)(2,1)S(1)}, u32[]{:S(2)}, u32[]{:S(2)}) collective-permute-start(bf16[2,8,64,256]{3,2,1,0:T(8,128)(2,1)S(1)} %collective-permute-done.13.refs_9_.refs_5_), channel_id=1, source_target_pairs={{0,1},{1,2},{2,3},{3,0},{4,5},{5,6},{6,7},{7,4},{8,9},{9,10},{10,1... | collective-permute-start | bytes 1572872 | tf_op jit(solution)/shard_map/ppermute | solution.py:354
  69.8 11.7 %copy-start.10 = (bf16[512,256]{1,0:T(8,128)(2,1)}, bf16[512,256]{1,0:T(8,128)(2,1)S(1)}, u32[]{:S(2)}) copy-start(bf16[512,256]{1,0:T(8,128)(2,1)S(1)} %collective-permute-done.19.refs_18_) | copy-start | bytes 786436
  74.7 6.8 %copy-start.11 = (bf16[512,256]{1,0:T(8,128)(2,1)}, bf16[512,256]{1,0:T(8,128)(2,1)S(1)}, u32[]{:S(2)}) copy-start(bf16[512,256]{1,0:T(8,128)(2,1)S(1)} %collective-permute-done.20.refs_19_) | copy-start | bytes 786436
  74.7 2.0 %collective-permute-start.21 = (bf16[512,256]{1,0:T(8,128)(2,1)S(1)}, bf16[512,256]{1,0:T(8,128)(2,1)S(1)}, u32[]{:S(2)}, u32[]{:S(2)}) collective-permute-start(bf16[512,256]{1,0:T(8,128)(2,1)S(1)} %collective-permute-done.19.refs_18_), channel_id=1, source_target_pairs={{0,4},{4,0},{8,12},{12,8},{16,20},{20,16},{24,28},{28,24},{32,36},... | collective-permute-start | bytes 786440 | tf_op jit(solution)/shard_map/ppermute | solution.py:379
  74.7 27.1 %collective-permute-start.17 = (bf16[1,8,64,256]{3,2,1,0:T(8,128)(2,1)}, bf16[1,8,64,256]{3,2,1,0:T(8,128)(2,1)S(1)}, u32[]{:S(2)}, u32[]{:S(2)}) collective-permute-start(bf16[1,8,64,256]{3,2,1,0:T(8,128)(2,1)} %get-tuple-element.39.refs_8_), channel_id=1, source_target_pairs={{0,3},{1,0},{2,1},{3,2},{4,7},{5,4},{6,5},{7,6},{8,11},{9,8},{10,9... | collective-permute-start | bytes 786440 | tf_op jit(solution)/shard_map/ppermute | solution.py:354
  76.7 4.7 %copy-start.12 = (bf16[512,256]{1,0:T(8,128)(2,1)}, bf16[512,256]{1,0:T(8,128)(2,1)S(1)}, u32[]{:S(2)}) copy-start(bf16[512,256]{1,0:T(8,128)(2,1)S(1)} %collective-permute-done.21.refs_17_) | copy-start | bytes 786436
  81.4 0.8 copy-start.8
  82.2 19.4 %copy-start.15 = (bf16[1,8,64,256]{3,2,1,0:T(8,128)(2,1)S(1)}, bf16[1,8,64,256]{3,2,1,0:T(8,128)(2,1)}, u32[]{:S(2)}) copy-start(bf16[1,8,64,256]{3,2,1,0:T(8,128)(2,1)} %get-tuple-element.39.refs_8_) | copy-start | bytes 786436
  86.9 17.6 %collective-permute-start.22 = (bf16[512,256]{1,0:T(8,128)(2,1)}, bf16[512,256]{1,0:T(8,128)(2,1)S(1)}, u32[]{:S(2)}, u32[]{:S(2)}) collective-permute-start(bf16[512,256]{1,0:T(8,128)(2,1)} %get-tuple-element.44.refs_20_), channel_id=1, source_target_pairs={{0,8},{4,12},{8,16},{12,20},{16,24},{20,28},{24,32},{28,36},{32,40... | collective-permute-start | bytes 786440 | tf_op jit(solution)/shard_map/ppermute | solution.py:359
  92.5 14.7 %collective-permute-start.23 = (bf16[512,256]{1,0:T(8,128)(2,1)}, bf16[512,256]{1,0:T(8,128)(2,1)S(1)}, u32[]{:S(2)}, u32[]{:S(2)}) collective-permute-start(bf16[512,256]{1,0:T(8,128)(2,1)} %get-tuple-element.44.refs_20_), channel_id=1, source_target_pairs={{0,4},{4,16},{8,12},{12,24},{16,20},{20,32},{24,28},{28,40},{32,36... | collective-permute-start | bytes 786440 | tf_op jit(solution)/shard_map/ppermute | solution.py:376
  101.7 6.5 %collective-permute-start.16 = (bf16[1,8,64,256]{3,2,1,0:T(8,128)(2,1)S(1)}, bf16[1,8,64,256]{3,2,1,0:T(8,128)(2,1)S(1)}, u32[]{:S(2)}, u32[]{:S(2)}) collective-permute-start(bf16[1,8,64,256]{3,2,1,0:T(8,128)(2,1)S(1)} %copy-done.15), channel_id=1, source_target_pairs={{0,1},{1,2},{2,3},{3,0},{4,5},{5,6},{6,7},{7,4},{8,9},{9,10},{10,1... | collective-permute-start | bytes 786440 | tf_op jit(solution)/shard_map/ppermute | solution.py:354
  101.8 7.0 %copy-start.16 = (bf16[1,8,64,256]{3,2,1,0:T(8,128)(2,1)}, bf16[1,8,64,256]{3,2,1,0:T(8,128)(2,1)S(1)}, u32[]{:S(2)}) copy-start(bf16[1,8,64,256]{3,2,1,0:T(8,128)(2,1)S(1)} %collective-permute-done.17.refs_10_) | copy-start | bytes 786436
  101.8 6.4 %collective-permute-start.18 = (bf16[1,8,64,256]{3,2,1,0:T(8,128)(2,1)S(1)}, bf16[1,8,64,256]{3,2,1,0:T(8,128)(2,1)S(1)}, u32[]{:S(2)}, u32[]{:S(2)}) collective-permute-start(bf16[1,8,64,256]{3,2,1,0:T(8,128)(2,1)S(1)} %collective-permute-done.17.refs_10_), channel_id=1, source_target_pairs={{0,3},{1,0},{2,1},{3,2},{4,7},{5,4},{6,5},{7,6},{8,11},{9,8},{10,9... | collective-permute-start | bytes 786440 | tf_op jit(solution)/shard_map/ppermute | solution.py:354
  104.4 4.3 %copy-start.17 = (bf16[512,256]{1,0:T(8,128)(2,1)}, bf16[512,256]{1,0:T(8,128)(2,1)S(1)}, u32[]{:S(2)}) copy-start(bf16[512,256]{1,0:T(8,128)(2,1)S(1)} %collective-permute-done.22.refs_22_) | copy-start | bytes 786436
  107.2 1.5 %copy-start.18 = (bf16[512,256]{1,0:T(8,128)(2,1)}, bf16[512,256]{1,0:T(8,128)(2,1)S(1)}, u32[]{:S(2)}) copy-start(bf16[512,256]{1,0:T(8,128)(2,1)S(1)} %collective-permute-done.23.refs_23_) | copy-start | bytes 786436
  107.2 1.5 %collective-permute-start.24 = (bf16[512,256]{1,0:T(8,128)(2,1)S(1)}, bf16[512,256]{1,0:T(8,128)(2,1)S(1)}, u32[]{:S(2)}, u32[]{:S(2)}) collective-permute-start(bf16[512,256]{1,0:T(8,128)(2,1)S(1)} %collective-permute-done.22.refs_22_), channel_id=1, source_target_pairs={{0,4},{4,0},{8,12},{12,8},{16,20},{20,16},{24,28},{28,24},{32,36},... | collective-permute-start | bytes 786440 | tf_op jit(solution)/shard_map/ppermute | solution.py:379
  108.2 0.7 copy-start.19
  108.2 0.8 copy-start.20
  (1 other events, 0.7 us)
